TPU v7x, 128 devices: a whole 4x4x4 slice. The times are simulated.
128 devices in a mesh: az: 8 (over z, x_lo), rg: 16 (over y, x_hi, core).
Axes of the slice: x: 4 (x_hi: 2, x_lo: 2; x = x_hi * 2 + x_lo), y: 4, z: 4, core: 2. Of those that a mesh axis runs over, the one named last changes fastest.
Arguments:
- slab_echoes: bfloat16 [2, 2048, 16384], P(None, ('az', 'rg')), may hold values from -6 to 6
- fresh_pulses: bfloat16 [2, 6144, 16384], P(None, ('az', 'rg')), may hold values from -6 to 6
- range_filter: float32 [2, 16384], replicated, may hold values from -5 to 5
- azimuth_filter: bfloat16 [2, 8192, 16384], P(None, None, ('az', 'rg')), may hold values from -5 to 5
- migration_taps: float32 [9, 8192], replicated, may hold values from -2.4 to 2.4
- band_offsets: int32 [16384], P(('az', 'rg')), may hold values from 0 to 56
- band_widths: int32 [16384], P(('az', 'rg')), may hold values from 1 to 9
Outputs:
- focused_image: bfloat16 [2, 6144, 16384], P(None, ('az', 'rg'))
All inputs are finite; a program needn't handle non-finite values.
Results may differ from a plain program's by a relative error of at most 0.019.
Values may be sent and summed in bfloat16 or wider, within the bound.
No kernel may reach another device: no remote copies, remote signals or barrier semaphores. Data moves between devices by JAX's collectives and lax.ppermute only.
A program may use at most 192 MiB of HBM per device.

v0:
```python
import math

import jax
import jax.numpy as jnp
from jax import lax
from jax.sharding import PartitionSpec as P

RANGE_OUTER = 128
RANGE_INNER = 128
PULSE_OUTER = 128
PULSE_INNER = 64
SLAB_PULSES = 2048
BAND_MAX = 9
RANGE_BINS = 16384
PULSES = 8192
FRESH_COUNT = 6144
RIM_WIDTH = 64


def passed_along(block, axis, distance):
    devices = range(lax.axis_size(axis))
    route = [(i - distance, i) for i in devices if i - distance in devices]
    return lax.ppermute(block, axis, route)


def dft_table(length, sign):
    index = jnp.arange(length, dtype=jnp.int32)
    angle = (index[:, None] * index[None, :] % length).astype(jnp.float32) * (
        2.0 * math.pi / length
    )
    scale = 1.0 / math.sqrt(length)
    real_part = jnp.cos(angle) * scale
    imag_part = sign * jnp.sin(angle) * scale
    upper = jnp.stack([real_part, imag_part], axis=1)
    lower = jnp.stack([-imag_part, real_part], axis=1)
    return jnp.stack([upper, lower], axis=0).astype(jnp.bfloat16)


def twiddle(rows_size, cols_size, total, sign):
    left = jnp.arange(rows_size, dtype=jnp.int32)[:, None]
    right = jnp.arange(cols_size, dtype=jnp.int32)[None, :]
    angle = (left * right % total).astype(jnp.float32) * (2.0 * math.pi / total)
    return (jnp.cos(angle), sign * jnp.sin(angle))


def complex_mul(values, real_part, imag_part):
    return jnp.stack(
        [
            values[0] * real_part - values[1] * imag_part,
            values[0] * imag_part + values[1] * real_part,
        ]
    )


def complex_mul_inner(values, real_part, imag_part):
    first = values[..., 0, :]
    second = values[..., 1, :]
    return jnp.stack(
        [first * real_part - second * imag_part, first * imag_part + second * real_part], axis=-2
    )


def range_compress(pulse_rows, range_filter):
    pulse_count = pulse_rows.shape[1]
    folded = pulse_rows.reshape(2, pulse_count, RANGE_OUTER, RANGE_INNER)
    partial_value = jnp.einsum(
        "cpab,cadk->pbdk", folded, dft_table(RANGE_OUTER, -1.0), preferred_element_type=jnp.float32
    )
    twist_re, twist_im = twiddle(RANGE_INNER, RANGE_OUTER, RANGE_BINS, -1.0)
    turned = complex_mul_inner(partial_value, twist_re, twist_im).astype(jnp.bfloat16)
    spectrum = jnp.einsum(
        "pbck,cbdm->pkdm", turned, dft_table(RANGE_INNER, -1.0), preferred_element_type=jnp.float32
    )
    shaped = range_filter.reshape(2, RANGE_INNER, RANGE_OUTER)
    matched = complex_mul_inner(spectrum, shaped[0].T, shaped[1].T).astype(jnp.bfloat16)
    inverse_part = jnp.einsum(
        "pkcm,cmdb->pkdb", matched, dft_table(RANGE_INNER, 1.0), preferred_element_type=jnp.float32
    )
    untwist_re, untwist_im = twiddle(RANGE_OUTER, RANGE_INNER, RANGE_BINS, 1.0)
    unturned = complex_mul_inner(inverse_part, untwist_re, untwist_im).astype(jnp.bfloat16)
    result = jnp.einsum(
        "pkcb,ckda->dpab", unturned, dft_table(RANGE_OUTER, 1.0), preferred_element_type=jnp.float32
    )
    return result.reshape(2, pulse_count, RANGE_BINS).astype(jnp.bfloat16)


def azimuth_forward(columns, filter_cols):
    local_bins = columns.shape[2]
    folded = columns.reshape(2, PULSE_OUTER, PULSE_INNER * local_bins)
    table = dft_table(PULSE_OUTER, -1.0)
    partial_value = jnp.einsum("cbx,cbdk->dkx", folded, table, preferred_element_type=jnp.float32)
    partial_value = partial_value.reshape(2, PULSE_OUTER, PULSE_INNER, local_bins)
    twist_re, twist_im = twiddle(PULSE_OUTER, PULSE_INNER, PULSES, -1.0)
    turned = complex_mul(partial_value, twist_re[:, :, None], twist_im[:, :, None]).astype(
        jnp.bfloat16
    )
    spectrum = jnp.einsum(
        "cklr,cldm->dmkr", turned, dft_table(PULSE_INNER, -1.0), preferred_element_type=jnp.float32
    )
    spectrum = spectrum.reshape(2, PULSES, local_bins)
    return complex_mul(
        spectrum, filter_cols[0].astype(jnp.float32), filter_cols[1].astype(jnp.float32)
    ).astype(jnp.bfloat16)


def azimuth_inverse(columns):
    local_bins = columns.shape[2]
    folded = columns.reshape(2, PULSE_INNER, PULSE_OUTER, local_bins)
    partial_value = jnp.einsum(
        "cmkr,cmdl->dlkr", folded, dft_table(PULSE_INNER, 1.0), preferred_element_type=jnp.float32
    )
    twist_re, twist_im = twiddle(PULSE_INNER, PULSE_OUTER, PULSES, 1.0)
    turned = complex_mul(partial_value, twist_re[:, :, None], twist_im[:, :, None]).astype(
        jnp.bfloat16
    )
    outer_table = dft_table(PULSE_OUTER, 1.0)[:, :, :, SLAB_PULSES // PULSE_INNER :]
    focused = jnp.einsum("clkr,ckdb->dblr", turned, outer_table, preferred_element_type=jnp.float32)
    return focused.reshape(2, FRESH_COUNT, local_bins).astype(jnp.bfloat16)


def migrate(extended, band_offsets, band_widths, migration_taps):
    local_bins = band_offsets.shape[0]
    block_cols = math.gcd(local_bins, 128)
    reach = block_cols + RIM_WIDTH
    column_ids = jnp.arange(reach, dtype=jnp.int32)[:, None]
    local_ids = jnp.arange(block_cols, dtype=jnp.int32)
    starts = local_ids + band_offsets
    total = jnp.zeros((2, PULSES, block_cols), jnp.float32)
    for tap_index in range(BAND_MAX):
        hits = (column_ids == (starts + tap_index)[None, :]) & (band_widths > tap_index)[None, :]
        selector = hits.astype(jnp.bfloat16)
        picked = jnp.einsum("cpe,en->cpn", extended, selector, preferred_element_type=jnp.float32)
        total = total + picked * migration_taps[tap_index][None, :, None]
    pieces = total.astype(jnp.bfloat16)
    return pieces


def on_device(
    slab_echoes,
    fresh_pulses,
    range_filter,
    azimuth_filter,
    migration_taps,
    band_offsets,
    band_widths,
):
    slab_done = range_compress(slab_echoes, range_filter)
    fresh_done = range_compress(fresh_pulses, range_filter)
    slab_turn, fresh_turn = (
        lax.all_to_all(slab_done, ("az", "rg"), split_axis=2, concat_axis=1, tiled=True),
        lax.all_to_all(fresh_done, ("az", "rg"), split_axis=2, concat_axis=1, tiled=True),
    )
    ordered = jnp.concatenate([slab_turn, fresh_turn], axis=1)
    spectra = azimuth_forward(ordered, azimuth_filter)
    edge_cols = passed_along(spectra[:, :, :RIM_WIDTH], ("az", "rg"), -1)
    extended = jnp.concatenate([spectra, edge_cols], axis=2)
    migrated = migrate(extended, band_offsets, band_widths, migration_taps)
    focused = azimuth_inverse(migrated)
    return lax.all_to_all(focused, ("az", "rg"), split_axis=1, concat_axis=2, tiled=True)


def solution(mesh):
    placed = (
        P(None, ("az", "rg"), None),
        P(None, ("az", "rg"), None),
        P(),
        P(None, None, ("az", "rg")),
        P(),
        P(("az", "rg")),
        P(("az", "rg")),
    )
    return jax.shard_map(
        on_device,
        mesh=mesh,
        in_specs=placed,
        out_specs=P(None, ("az", "rg"), None),
        check_vma=False,
    )
```

profile of v0, /device:TPU:1, one launch (start us, length us, event | category | flops | bytes accessed | tf_op | source)
XLA Modules:
  0.0 450.7 jit_solution(15252405704241671842)
XLA Ops:
  1.4 1.5 copy.220
  2.9 1.1 fusion.174
  4.2 0.4 convolution_bitcast_fusion.3
  4.9 0.5 convolution_bitcast_fusion.2
  5.7 0.5 convolution_bitcast_fusion.1
  6.5 0.5 fusion.56
  7.0 9.2 %copy.204 = bf16[2,16,128,128]{1,0,3,2:T(2,128)(2,1)} copy(bf16[2,16,128,128]{3,2,1,0:T(8,128)(2,1)S(1)} %fusion.56) | data formatting | bytes 2097152 | tf_op jit(solution)/shard_map/convert_element_type | solution.py:84
  16.2 24.0 %reshape.480 = bf16[128,2,2048]{2,1,0:T(2,128)(2,1)} reshape(bf16[16384,2,16]{2,1,0:T(2,128)(2,1)} %bitcast.302) | data formatting | bytes 2097152
  40.1 11.8 %all-to-all-start = ((bf16[128,2,2048]{2,1,0:T(2,128)(2,1)}), bf16[128,2,2048]{2,1,0:T(2,128)(2,1)S(1)}, u32[]{:S(2)}, u32[]{:S(2)}) async-start(bf16[128,2,2048]{2,1,0:T(2,128)(2,1)} %reshape.480), calls=%async_computation | async-start | bytes 2097152 | tf_op jit(solution)/shard_map/all_to_all | solution.py:150
  52.0 2.8 copy.221
  54.7 1.0 fusion.46
  55.7 0.9 subtract_convert_fusion.3
  56.7 1.0 fusion.49
  57.7 0.9 subtract_convert_fusion.2
  58.6 1.0 fusion.45
  59.6 0.9 subtract_convert_fusion.1
  60.5 2.7 fusion.34
  63.2 14.2 %copy.216 = bf16[2,48,128,128]{1,0,3,2:T(2,128)(2,1)} copy(bf16[2,48,128,128]{3,2,1,0:T(8,128)(2,1)} %fusion.34) | data formatting | bytes 6291456 | tf_op jit(solution)/shard_map/convert_element_type | solution.py:84
  77.3 29.8 %reshape.478 = bf16[128,2,6144]{2,1,0:T(2,128)(2,1)} reshape(bf16[16384,2,48]{2,1,0:T(2,128)(2,1)} %bitcast.304) | data formatting | bytes 6291456
  107.2 1.0 copy-done.1
  108.1 9.8 %all-to-all-start.1 = ((bf16[128,2,6144]{2,1,0:T(2,128)(2,1)}), bf16[128,2,6144]{2,1,0:T(2,128)(2,1)S(1)}, u32[]{:S(2)}, u32[]{:S(2)}) async-start(bf16[128,2,6144]{2,1,0:T(2,128)(2,1)} %reshape.478), calls=%async_computation.1 | async-start | bytes 6291456 | tf_op jit(solution)/shard_map/all_to_all | solution.py:151
  117.9 4.5 fusion.172
  122.4 4.1 copy.217
  126.5 4.1 copy.218
  131.3 0.7 fusion.153
  132.0 0.6 broadcast_compare_fusion.8
  132.6 26.4 %reshape.481 = bf16[16384,2,16]{2,1,0:T(2,128)(2,1)} reshape(bf16[128,2,2048]{2,1,0:T(2,128)(2,1)} %copy-done.1) | data formatting | bytes 2097152
  159.0 16.5 %copy.132 = bf16[2,128,16,128]{3,2,1,0:T(8,128)(2,1)} copy(bf16[2,128,16,128]{2,0,3,1:T(2,128)(2,1)} %bitcast.303) | data formatting | bytes 2097152 | tf_op jit(solution)/shard_map/all_to_all | solution.py:150
  175.5 9.4 %reshape.479 = bf16[16384,2,48]{2,1,0:T(2,128)(2,1)} reshape(bf16[128,2,6144]{2,1,0:T(2,128)(2,1)S(1)} %all-to-all-done.1) | data formatting | bytes 6291456
  184.9 16.0 %copy.142 = bf16[2,128,48,128]{3,2,1,0:T(8,128)(2,1)S(1)} copy(bf16[2,128,48,128]{2,0,3,1:T(2,128)(2,1)} %bitcast.305) | data formatting | bytes 6291456 | tf_op jit(solution)/shard_map/all_to_all | solution.py:151
  200.9 3.5 pad_maximum_fusion.1
  204.4 7.3 %reshape.457 = bf16[2,128,8192,1]{2,1,0,3:T(8,128)(2,1)} reshape(bf16[2,8192,128]{2,1,0:T(8,128)(2,1)} %pad_maximum_fusion.1) | data formatting | bytes 8388608 | tf_op jit(solution)/shard_map/reshape | solution.py:89
  211.7 3.4 convolution_bitcast_fusion
  215.1 0.9 slice_bitcast_fusion.1
  216.0 0.7 copy.223
  216.8 0.7 copy.222
  217.6 4.0 fusion.16
  221.6 1.3 fusion.33
  222.9 3.3 fusion.171
  226.1 4.5 copy.147
  230.6 5.6 %copy.149 = f32[1,8192,128]{1,2,0:T(8,128)} copy(f32[1,8192,128]{2,1,0:T(8,128)} %bitcast.310) | data formatting | bytes 8388608 | tf_op jit(solution)/shard_map/squeeze | solution.py:49
  236.2 6.6 %copy.150 = f32[1,64,128,128]{3,2,1,0:T(8,128)} copy(f32[1,64,128,128]{3,1,2,0:T(8,128)} %get-tuple-element.12) | data formatting | bytes 8388608 | tf_op jit(solution)/shard_map/slice | solution.py:49
  242.9 5.6 %copy.152 = f32[1,8192,128]{1,2,0:T(8,128)} copy(f32[1,8192,128]{2,1,0:T(8,128)} %bitcast.311) | data formatting | bytes 8388608 | tf_op jit(solution)/shard_map/squeeze | solution.py:49
  248.5 6.0 %fusion.10 = (bf16[1,8192,128]{1,2,0:T(8,128)(2,1)S(1)}, bf16[1,8192,128]{1,2,0:T(8,128)(2,1)S(1)}) fusion(f32[1,8192,128]{1,2,0:T(8,128)} %copy.149, bf16[1,8192,128]{1,2,0:T(8,128)(2,1)} %copy.217, f32[1,8192,128]{1,2,0:T(8,128)} %copy.152, bf16[1,8192,128]{1,2,0:T(8,128)(2,1)} %copy.218), kind=kLoop, calls=%fused_computation.27 | loop fusion | flops 10485760 | bytes 16777216 | tf_op jit(solution)/shard_map/convert.2
  254.7 3.1 collective-permute-start
  258.3 25.4 %collective-permute-done = bf16[2,8192,64]{1,2,0:T(8,128)(2,1)S(1)} collective-permute-done((bf16[2,8192,64]{1,2,0:T(8,128)(2,1)S(1)}, bf16[2,8192,64]{1,2,0:T(8,128)(2,1)S(1)}, u32[]{:S(2)}, u32[]{:S(2)}) %collective-permute-start) | collective-permute-done | bytes 2097184 | tf_op jit(solution)/shard_map/ppermute | solution.py:23
  283.7 5.8 %convolution_multiply_fusion.7 = f32[2,8192,128]{2,1,0:T(8,128)} fusion(f32[8192]{0:T(1024)S(1)} %bitcast.333, s32[128]{0:T(128)S(1)} %get-tuple-element.58, pred[128]{0:T(512)(128)(4,1)S(1)} %copy-done.15, bf16[2,8192,64]{1,2,0:T(8,128)(2,1)S(1)} %collective-permute-done, bf16[1,8192,128]{1,2,0:T(8,128)(2,1)S(1)} %get-tuple-element.6, ...), kind=kOutput, calls=%fused_computation.8 | convolution fusion | flops 826327040 | bytes 14713472 | tf_op jit(solution)/shard_map/cpe,en->cpn/dot_general | solution.py:132
  289.5 5.5 %convolution_multiply_fusion.6 = f32[2,8192,128]{2,1,0:T(8,128)} fusion(f32[8192]{0:T(1024)S(1)} %bitcast.332, s32[128]{0:T(128)S(1)} %get-tuple-element.59, pred[128]{0:T(512)(128)(4,1)S(1)} %copy-done.14, bf16[2,8192,64]{1,2,0:T(8,128)(2,1)S(1)} %collective-permute-done, bf16[1,8192,128]{1,2,0:T(8,128)(2,1)S(1)} %get-tuple-element.6, ...), kind=kOutput, calls=%fused_computation.7 | convolution fusion | flops 826327040 | bytes 14713472 | tf_op jit(solution)/shard_map/cpe,en->cpn/dot_general | solution.py:132
  295.0 5.6 %convolution_multiply_fusion.5 = f32[2,8192,128]{2,1,0:T(8,128)} fusion(f32[8192]{0:T(1024)S(1)} %bitcast.331, s32[128]{0:T(128)S(1)} %get-tuple-element.60, pred[128]{0:T(512)(128)(4,1)S(1)} %copy-done.13, bf16[2,8192,64]{1,2,0:T(8,128)(2,1)S(1)} %collective-permute-done, bf16[1,8192,128]{1,2,0:T(8,128)(2,1)S(1)} %get-tuple-element.6, ...), kind=kOutput, calls=%fused_computation.6 | convolution fusion | flops 826327040 | bytes 14713472 | tf_op jit(solution)/shard_map/cpe,en->cpn/dot_general | solution.py:132
  300.5 5.5 %convolution_multiply_fusion.4 = f32[2,8192,128]{2,1,0:T(8,128)} fusion(f32[8192]{0:T(1024)S(1)} %bitcast.330, s32[128]{0:T(128)S(1)} %get-tuple-element.61, pred[128]{0:T(512)(128)(4,1)S(1)} %copy-done.12, bf16[2,8192,64]{1,2,0:T(8,128)(2,1)S(1)} %collective-permute-done, bf16[1,8192,128]{1,2,0:T(8,128)(2,1)S(1)} %get-tuple-element.6, ...), kind=kOutput, calls=%fused_computation.5 | convolution fusion | flops 826327040 | bytes 14713472 | tf_op jit(solution)/shard_map/cpe,en->cpn/dot_general | solution.py:132
  306.0 5.5 %convolution_multiply_fusion.3 = f32[2,8192,128]{2,1,0:T(8,128)} fusion(f32[8192]{0:T(1024)S(1)} %bitcast.329, s32[128]{0:T(128)S(1)} %get-tuple-element.62, pred[128]{0:T(512)(128)(4,1)S(1)} %copy-done.11, bf16[2,8192,64]{1,2,0:T(8,128)(2,1)S(1)} %collective-permute-done, bf16[1,8192,128]{1,2,0:T(8,128)(2,1)S(1)} %get-tuple-element.6, ...), kind=kOutput, calls=%fused_computation.4 | convolution fusion | flops 826327040 | bytes 14713472 | tf_op jit(solution)/shard_map/cpe,en->cpn/dot_general | solution.py:132
  311.6 5.5 %convolution_multiply_fusion.2 = f32[2,8192,128]{2,1,0:T(8,128)} fusion(f32[8192]{0:T(1024)S(1)} %bitcast.328, s32[128]{0:T(128)S(1)} %get-tuple-element.63, pred[128]{0:T(512)(128)(4,1)S(1)} %copy-done.10, bf16[2,8192,64]{1,2,0:T(8,128)(2,1)S(1)} %collective-permute-done, bf16[1,8192,128]{1,2,0:T(8,128)(2,1)S(1)} %get-tuple-element.6, ...), kind=kOutput, calls=%fused_computation.3 | convolution fusion | flops 826327040 | bytes 14713472 | tf_op jit(solution)/shard_map/cpe,en->cpn/dot_general | solution.py:132
  317.0 5.5 %convolution_multiply_fusion.1 = f32[2,8192,128]{2,1,0:T(8,128)} fusion(f32[8192]{0:T(1024)S(1)} %bitcast.327, s32[128]{0:T(128)S(1)} %get-tuple-element.64, pred[128]{0:T(512)(128)(4,1)S(1)} %get-tuple-element.56, bf16[2,8192,64]{1,2,0:T(8,128)(2,1)S(1)} %collective-permute-done, bf16[1,8192,128]{1,2,0:T(8,128)(2,1)S(1)} %get-tuple-element.6, ...), kind=kOutput, calls=%fused_computation.2 | convolution fusion | flops 826327040 | bytes 14713472 | tf_op jit(solution)/shard_map/cpe,en->cpn/dot_general | solution.py:132
  322.6 5.5 %convolution_multiply_fusion = f32[2,8192,128]{2,1,0:T(8,128)} fusion(f32[8192]{0:T(1024)S(1)} %bitcast.326, s32[128]{0:T(128)S(1)} %get-tuple-element.65, pred[128]{0:T(512)(128)(4,1)S(1)} %get-tuple-element.55, bf16[2,8192,64]{1,2,0:T(8,128)(2,1)S(1)} %collective-permute-done, bf16[1,8192,128]{1,2,0:T(8,128)(2,1)S(1)} %get-tuple-element.6, ...), kind=kOutput, calls=%fused_computation.1 | convolution fusion | flops 826327040 | bytes 14713472 | tf_op jit(solution)/shard_map/cpe,en->cpn/dot_general | solution.py:132
  328.1 26.2 %fusion.8 = bf16[2,8192,128]{2,1,0:T(8,128)(2,1)} fusion(f32[2,8192,128]{2,1,0:T(8,128)} %convolution_multiply_fusion, f32[2,8192,128]{2,1,0:T(8,128)} %convolution_multiply_fusion.1, f32[2,8192,128]{2,1,0:T(8,128)} %convolution_multiply_fusion.2, f32[2,8192,128]{2,1,0:T(8,128)} %convolution_multiply_fusion.3, ...), kind=kOutput, calls=%fused_computation.18 | convolution fusion | flops 845201408 | bytes 77628032 | tf_op jit(solution)/shard_map/cpe,en->cpn/dot_general | solution.py:132
  354.3 5.4 %fusion.30 = f32[2,64,128,128]{3,1,2,0:T(8,128)S(1)} fusion(bf16[2,64,128,128]{3,2,1,0:T(8,128)(2,1)} %bitcast.306, bf16[1,64,2,64]{1,3,2,0:T(8,128)(2,1)S(1)} %copy-done.5, bf16[1,64,2,64]{1,3,2,0:T(8,128)(2,1)S(1)} %copy-done.4), kind=kOutput, calls=%fused_computation.56 | convolution fusion | flops 536887296 | bytes 12615680 | tf_op jit(solution)/shard_map/cmkr,cmdl->dlkr/dot_general | solution.py:109
  359.7 3.6 subtract_convert_fusion
  363.3 0.4 pad_maximum_fusion.2
  363.6 3.1 bitcast_convert_fusion
  366.7 1.2 copy.159
  367.9 26.7 %copy.160 = bf16[2,6144,128]{2,0,1:T(2,128)(2,1)S(1)} copy(bf16[2,6144,128]{2,1,0:T(8,128)(2,1)S(1)} %bitcast.312) | data formatting | bytes 6291456 | tf_op jit(solution)/shard_map/convert_element_type | solution.py:118
  394.6 52.8 %all_to_all.54 = bf16[2,6144,128]{2,0,1:T(2,128)(2,1)S(1)} all-to-all(bf16[2,6144,128]{2,0,1:T(2,128)(2,1)S(1)} %copy.160), channel_id=1, replica_groups=mesh['az'=8,'rg'=16] {'az','rg'}, dimensions={1} | all-to-all | bytes 6291456 | tf_op jit(solution)/shard_map/all_to_all | solution.py:159
  447.5 0.4 copy.161
  447.9 2.4 copy.271
  (52 shorter events, 3.9 us)
Async XLA Ops:
  40.1 67.0 %all-to-all-start = ((bf16[128,2,2048]{2,1,0:T(2,128)(2,1)}), bf16[128,2,2048]{2,1,0:T(2,128)(2,1)S(1)}, u32[]{:S(2)}, u32[]{:S(2)}) async-start(bf16[128,2,2048]{2,1,0:T(2,128)(2,1)} %reshape.480), calls=%async_computation | async-start | bytes 2097152 | tf_op jit(solution)/shard_map/all_to_all | solution.py:150
  107.2 1.0 copy-start.1
  108.1 67.4 %all-to-all-start.1 = ((bf16[128,2,6144]{2,1,0:T(2,128)(2,1)}), bf16[128,2,6144]{2,1,0:T(2,128)(2,1)S(1)}, u32[]{:S(2)}, u32[]{:S(2)}) async-start(bf16[128,2,6144]{2,1,0:T(2,128)(2,1)} %reshape.478), calls=%async_computation.1 | async-start | bytes 6291456 | tf_op jit(solution)/shard_map/all_to_all | solution.py:151
  122.4 9.6 %copy-start.8 = (s32[128]{0:T(128)S(1)}, s32[128]{0:T(128)}, u32[]{:S(2)}) copy-start(s32[128]{0:T(128)} %param.13) | copy-start | bytes 1540
  217.5 4.0 copy-start.6
  217.5 4.0 copy-start.7
  254.5 68.1 %copy-start = (bf16[1,8192,128]{1,2,0:T(8,128)(2,1)}, bf16[1,8192,128]{1,2,0:T(8,128)(2,1)S(1)}, u32[]{:S(2)}) copy-start(bf16[1,8192,128]{1,2,0:T(8,128)(2,1)S(1)} %get-tuple-element.6) | copy-start | bytes 6291460
  254.5 3.6 copy-start.9
  254.5 3.6 copy-start.3
  254.5 29.2 %copy-start.15 = (pred[128]{0:T(512)(128)(4,1)S(1)}, pred[128]{0:T(512)(128)(4,1)}, u32[]{:S(2)}) copy-start(pred[128]{0:T(512)(128)(4,1)} %get-tuple-element.54) | copy-start | bytes 388
  254.7 29.0 %collective-permute-start = (bf16[2,8192,64]{1,2,0:T(8,128)(2,1)S(1)}, bf16[2,8192,64]{1,2,0:T(8,128)(2,1)S(1)}, u32[]{:S(2)}, u32[]{:S(2)}) collective-permute-start(bf16[2,8192,64]{1,2,0:T(8,128)(2,1)S(1)} %pad_maximum_fusion.3), channel_id=1, source_target_pairs={{1,0},{2,1},{3,2},{4,3},{5,4},{6,5},{7,6},{8,7},{9,8},{10,9},{11,1... | collective-permute-start | bytes 6291464 | tf_op jit(solution)/shard_map/ppermute | solution.py:23
  283.7 38.9 %copy-start.2 = (bf16[2,8192,64]{1,2,0:T(8,128)(2,1)}, bf16[2,8192,64]{1,2,0:T(8,128)(2,1)S(1)}, u32[]{:S(2)}) copy-start(bf16[2,8192,64]{1,2,0:T(8,128)(2,1)S(1)} %collective-permute-done) | copy-start | bytes 6291460
  283.7 5.8 %copy-start.14 = (pred[128]{0:T(512)(128)(4,1)S(1)}, pred[128]{0:T(512)(128)(4,1)}, u32[]{:S(2)}) copy-start(pred[128]{0:T(512)(128)(4,1)} %get-tuple-element.53) | copy-start | bytes 388
  289.5 5.5 %copy-start.13 = (pred[128]{0:T(512)(128)(4,1)S(1)}, pred[128]{0:T(512)(128)(4,1)}, u32[]{:S(2)}) copy-start(pred[128]{0:T(512)(128)(4,1)} %get-tuple-element.52) | copy-start | bytes 388
  295.0 5.6 %copy-start.12 = (pred[128]{0:T(512)(128)(4,1)S(1)}, pred[128]{0:T(512)(128)(4,1)}, u32[]{:S(2)}) copy-start(pred[128]{0:T(512)(128)(4,1)} %get-tuple-element.51) | copy-start | bytes 388
  300.5 5.5 %copy-start.11 = (pred[128]{0:T(512)(128)(4,1)S(1)}, pred[128]{0:T(512)(128)(4,1)}, u32[]{:S(2)}) copy-start(pred[128]{0:T(512)(128)(4,1)} %get-tuple-element.50) | copy-start | bytes 388
  306.0 5.5 %copy-start.10 = (pred[128]{0:T(512)(128)(4,1)S(1)}, pred[128]{0:T(512)(128)(4,1)}, u32[]{:S(2)}) copy-start(pred[128]{0:T(512)(128)(4,1)} %get-tuple-element.49) | copy-start | bytes 388
  328.1 26.2 %copy-start.4 = (bf16[1,64,2,64]{1,3,2,0:T(8,128)(2,1)S(1)}, bf16[1,64,2,64]{1,3,2,0:T(8,128)(2,1)}, u32[]{:S(2)}) copy-start(bf16[1,64,2,64]{1,3,2,0:T(8,128)(2,1)} %get-tuple-element.44) | copy-start | bytes 49156
  328.1 26.2 %copy-start.5 = (bf16[1,64,2,64]{1,3,2,0:T(8,128)(2,1)S(1)}, bf16[1,64,2,64]{1,3,2,0:T(8,128)(2,1)}, u32[]{:S(2)}) copy-start(bf16[1,64,2,64]{1,3,2,0:T(8,128)(2,1)} %get-tuple-element.47) | copy-start | bytes 49156
where the time goes:
time: 459 us; the launch traced here: 451 us
  local copies, waits for them, and re-layouts  231 us (50%)
  matrix products  91.3 us (20%)
  blocking collectives  52.8 us (12%)
  waiting for transfers between devices  25.4 us (6%)
  other arithmetic  24.8 us (5%)
  starting transfers between devices  24.7 us (5%)
    unnamed x43, local copies, waits for them, and re-layouts  105 us
    dot_general x9, matrix products, migrate(): jnp.einsum('cpe,en->cpn', extended, selector, preferred_element_type=jnp....  70.5 us
    all_to_all x1, blocking collectives, on_device(): lax.all_to_all(focused, ('az', 'rg'), split_axis=1, concat_axis=2, tiled=...  52.8 us
    convert_element_type x2, local copies, waits for them, and re-layouts, azimuth_inverse(): return focused.reshape(2, FRESH_COUNT, local_bins).astype(jnp.bfloat16)  27.9 us
    ppermute x1, waiting for transfers between devices, passed_along(): return lax.ppermute(block, axis, route)  25.4 us
    convert_element_type x2, local copies, waits for them, and re-layouts, range_compress(): return result.reshape(2, pulse_count, RANGE_BINS).astype(jnp.bfloat16)  23.4 us
    another operation x15, other arithmetic  18.4 us
    all_to_all x1, local copies, waits for them, and re-layouts, on_device(): lax.all_to_all(slab_done, ('az', 'rg'), split_axis=2, concat_axis=1, tile...  16.5 us
  transfers between devices with their start and end apart: 3, of which 1 were waited for; matrix products, arithmetic and copies ran while one was open for 25% of the time, Pallas kernels for 0%

commit v1 on v0

v1 whole, which is shorter than its diff:
```python
import functools
import math

import jax
import jax.numpy as jnp
import ml_dtypes
import numpy as np
from jax import lax
from jax.experimental import pallas as pl
from jax.experimental.pallas import tpu as pltpu
from jax.sharding import PartitionSpec as P

RANGE_OUTER = 128
RANGE_INNER = 128
PULSE_OUTER = 128
PULSE_INNER = 64
SLAB_PULSES = 2048
BAND_MAX = 9
RANGE_BINS = 16384
PULSES = 8192
FRESH_COUNT = 6144
LANES = 128
HALF = 64
DEVICES = 128
SLAB_ROWS = SLAB_PULSES // DEVICES
FRESH_ROWS = FRESH_COUNT // DEVICES
ROWS = SLAB_ROWS + FRESH_ROWS
STEP = 16
FIRST_OUTER = SLAB_PULSES // PULSE_INNER
KEPT_OUTER = PULSE_OUTER - FIRST_OUTER
GROUP = 4
AXES = ("az", "rg")
MIB = 1024 * 1024


def bf16(values):
    return np.asarray(values, np.float32).astype(ml_dtypes.bfloat16)


def dft_table(length, sign):
    index = np.arange(length)
    angle = (np.outer(index, index) % length).astype(np.float32) * np.float32(
        2.0 * math.pi / length
    )
    scale = np.float32(1.0 / math.sqrt(length))
    real_part = bf16(np.cos(angle) * scale).astype(np.float32)
    imag_part = bf16(sign * np.sin(angle) * scale).astype(np.float32)
    return real_part, imag_part


def twiddle(rows_size, cols_size, total, sign):
    angle = (np.outer(np.arange(rows_size), np.arange(cols_size)) % total).astype(
        np.float32
    ) * np.float32(2.0 * math.pi / total)
    return np.cos(angle), np.float32(sign) * np.sin(angle)


def left_table(length, sign):
    re, im = dft_table(length, sign)
    return bf16(np.block([[re, -im], [im, re]]))


def right_table(length, sign):
    re, im = dft_table(length, sign)
    return bf16(np.block([[re, im], [-im, re]]))


def turned_tables(outer, inner, sign):
    re, im = dft_table(outer, sign)
    tw_re, tw_im = twiddle(outer, inner, PULSES, sign)
    turn_re, turn_im = tw_re.T[:, :, None], tw_im.T[:, :, None]
    return bf16(
        np.concatenate(
            [re * turn_re - im * turn_im, re * turn_im + im * turn_re], axis=2
        )
    )


def roll_half(values):
    return pltpu.roll(values, HALF, 1)


def lane_ids(rows):
    return lax.broadcasted_iota(jnp.int32, (rows, LANES), 1)


def times_i(values):
    turned = roll_half(values)
    return jnp.where(lane_ids(values.shape[0]) < HALF, -turned, turned)


def dot(left, right):
    return jnp.dot(left, right, preferred_element_type=jnp.float32)


def range_kernel(slab, fresh, filt, t1, t2, t3, t4, w_in, w_out, out0, out1, xs, os, hs):
    step = pl.program_id(0)

    def load(source):
        def one(n1, _):
            at = pl.ds(pl.multiple_of(n1 * LANES, LANES), LANES)
            to = pl.ds(pl.multiple_of(n1 * STEP, STEP), STEP)
            for c in range(2):
                xs[c, to, :] = source[c, :, at].astype(jnp.float32)
            return 0

        lax.fori_loop(0, RANGE_OUTER, one, 0, unroll=8)

    @pl.when(step == 0)
    def _():
        hs[0] = filt[0].T
        hs[1] = filt[1].T
        load(slab)

    @pl.when(step > 0)
    def _():
        load(fresh)

    def rows(p):
        return pl.ds(p, RANGE_OUTER, stride=STEP)

    def pair(i, _):
        ps = (2 * i, 2 * i + 1)
        x = jnp.concatenate(
            [
                jnp.concatenate([xs[c, rows(p), :].astype(jnp.bfloat16) for p in ps], axis=1)
                for c in range(2)
            ],
            axis=0,
        )
        y = dot(t1[...], x)
        parts = []
        for k in range(2):
            re, im = y[:LANES, k * LANES : (k + 1) * LANES], y[LANES:, k * LANES : (k + 1) * LANES]
            parts.append(
                jnp.concatenate(
                    [
                        (re * w_in[0] - im * w_in[1]).astype(jnp.bfloat16),
                        (re * w_in[1] + im * w_in[0]).astype(jnp.bfloat16),
                    ],
                    axis=1,
                )
            )
        y = dot(jnp.concatenate(parts, axis=0), t2[...])
        parts = []
        for k in range(2):
            re, im = y[k * LANES : (k + 1) * LANES, :LANES], y[k * LANES : (k + 1) * LANES, LANES:]
            parts.append(
                jnp.concatenate(
                    [
                        (re * hs[0] - im * hs[1]).astype(jnp.bfloat16),
                        (re * hs[1] + im * hs[0]).astype(jnp.bfloat16),
                    ],
                    axis=1,
                )
            )
        y = dot(jnp.concatenate(parts, axis=0), t3[...])
        parts = []
        for k in range(2):
            re, im = y[k * LANES : (k + 1) * LANES, :LANES], y[k * LANES : (k + 1) * LANES, LANES:]
            parts.append(
                jnp.concatenate(
                    [
                        (re * w_out[0] - im * w_out[1]).astype(jnp.bfloat16),
                        (re * w_out[1] + im * w_out[0]).astype(jnp.bfloat16),
                    ],
                    axis=0,
                )
            )
        y = dot(t4[...], jnp.concatenate(parts, axis=1))
        low = lane_ids(LANES) < HALF
        for k, p in enumerate(ps):
            re, im = y[:LANES, k * LANES : (k + 1) * LANES], y[LANES:, k * LANES : (k + 1) * LANES]
            os[0, rows(p), :] = jnp.where(low, re, roll_half(im))
            os[1, rows(p), :] = jnp.where(low, roll_half(re), im)
        return 0

    lax.fori_loop(0, STEP // 2, pair, 0)

    def store(n1, _):
        at = pl.ds(pl.multiple_of(n1 * STEP, STEP), STEP)
        out0[n1] = os[0, at, :].astype(jnp.bfloat16)
        out1[n1] = os[1, at, :].astype(jnp.bfloat16)
        return 0

    lax.fori_loop(0, RANGE_OUTER, store, 0, unroll=8)


def whole(shape):
    return pl.BlockSpec(shape, lambda *_: (0,) * len(shape))


def range_compress(slab, fresh, range_filter):
    filt = range_filter.reshape(2, RANGE_INNER, RANGE_OUTER)
    tables = (
        left_table(RANGE_OUTER, -1.0),
        right_table(RANGE_INNER, -1.0),
        right_table(RANGE_INNER, 1.0),
        left_table(RANGE_OUTER, 1.0),
    )
    w_in = np.stack(twiddle(RANGE_OUTER, RANGE_INNER, RANGE_BINS, -1.0))
    w_out = np.stack(twiddle(RANGE_OUTER, RANGE_INNER, RANGE_BINS, 1.0))
    square = whole((2 * LANES, 2 * LANES))
    part = whole((2, LANES, LANES))
    out = jax.ShapeDtypeStruct((DEVICES, ROWS, LANES), jnp.bfloat16)
    return pl.pallas_call(
        range_kernel,
        grid=(ROWS // STEP,),
        in_specs=[
            whole((2, STEP, RANGE_BINS)),
            pl.BlockSpec((2, STEP, RANGE_BINS), lambda i: (0, jnp.maximum(i - 1, 0), 0)),
            part,
            square,
            square,
            square,
            square,
            part,
            part,
        ],
        out_specs=[pl.BlockSpec((DEVICES, STEP, LANES), lambda i: (0, i, 0))] * 2,
        out_shape=[out, out],
        scratch_shapes=[
            pltpu.VMEM((2, RANGE_OUTER * STEP, LANES), jnp.float32),
            pltpu.VMEM((2, RANGE_OUTER * STEP, LANES), jnp.float32),
            pltpu.VMEM((2, LANES, LANES), jnp.float32),
        ],
        compiler_params=pltpu.CompilerParams(
            dimension_semantics=("arbitrary",), vmem_limit_bytes=32 * MIB
        ),
        cost_estimate=pl.CostEstimate(
            flops=4 * 2 * ROWS * RANGE_BINS * 512, bytes_accessed=8 * MIB, transcendentals=0
        ),
        name="range_compress",
    )(slab, fresh, filt, *tables, w_in, w_out)


def filter_kernel(filt, out, fs):
    for c in range(2):
        for kl in range(PULSE_INNER):
            fs[c, kl * STEP : (kl + 1) * STEP, :] = filt[c, kl].astype(jnp.float32)
    low = lane_ids(PULSE_INNER) < HALF
    for kb in range(STEP):
        for c in range(2):
            value = fs[c, pl.ds(kb, PULSE_INNER, stride=STEP), :]
            turned = roll_half(value)
            at = slice(kb * PULSE_INNER, (kb + 1) * PULSE_INNER)
            out[0, c, at, :] = jnp.where(low, value, turned).astype(jnp.bfloat16)
            out[1, c, at, :] = jnp.where(low, turned, value).astype(jnp.bfloat16)


def filter_by_outer(azimuth_filter):
    folded = azimuth_filter.reshape(2, PULSE_INNER, PULSE_OUTER, LANES)
    return pl.pallas_call(
        filter_kernel,
        grid=(PULSE_OUTER // STEP,),
        in_specs=[pl.BlockSpec((2, PULSE_INNER, STEP, LANES), lambda i: (0, 0, i, 0))],
        out_specs=pl.BlockSpec((2, 2, STEP * PULSE_INNER, LANES), lambda i: (0, 0, i, 0)),
        out_shape=jax.ShapeDtypeStruct((2, 2, PULSES, LANES), jnp.bfloat16),
        scratch_shapes=[pltpu.VMEM((2, PULSE_INNER * STEP, LANES), jnp.float32)],
        compiler_params=pltpu.CompilerParams(
            dimension_semantics=("arbitrary",), vmem_limit_bytes=24 * MIB
        ),
        cost_estimate=pl.CostEstimate(
            flops=8 * PULSES * LANES, bytes_accessed=12 * MIB, transcendentals=0
        ),
        name="filter_by_outer",
    )(folded)


def forward_kernel(got, g1, t2, filt, out, ps, ts):
    def unpack(s, _):
        block = got[s].astype(jnp.float32)
        ps[pl.ds(pl.multiple_of(s * SLAB_ROWS, SLAB_ROWS), SLAB_ROWS), :] = block[:SLAB_ROWS]
        at = pl.multiple_of(SLAB_PULSES + s * FRESH_ROWS, STEP)
        ps[pl.ds(at, FRESH_ROWS), :] = block[SLAB_ROWS:]
        return 0

    lax.fori_loop(0, DEVICES, unpack, 0, unroll=4)

    def outer(l, _):
        x = ps[pl.ds(l, PULSE_OUTER, stride=PULSE_INNER), :]
        both = jnp.concatenate([x.astype(jnp.bfloat16), times_i(x).astype(jnp.bfloat16)], axis=0)
        ts[pl.ds(l, PULSE_OUTER, stride=PULSE_INNER), :] = dot(g1[l], both)
        return 0

    lax.fori_loop(0, PULSE_INNER, outer, 0, unroll=4)

    def inner(i, _):
        sides = []
        for k in range(2):
            at = pl.ds(pl.multiple_of((2 * i + k) * PULSE_INNER, PULSE_INNER), PULSE_INNER)
            t = ts[at, :]
            sides.append(
                jnp.concatenate([t.astype(jnp.bfloat16), times_i(t).astype(jnp.bfloat16)], axis=0)
            )
        y = dot(t2[...], jnp.concatenate(sides, axis=1))
        for k in range(2):
            at = pl.ds(pl.multiple_of((2 * i + k) * PULSE_INNER, PULSE_INNER), PULSE_INNER)
            cols = slice(k * LANES, (k + 1) * LANES)
            out[at, :] = (
                y[:PULSE_INNER, cols] * filt[0, 0, at, :].astype(jnp.float32)
                + y[PULSE_INNER:, cols] * filt[0, 1, at, :].astype(jnp.float32)
            ).astype(jnp.bfloat16)
        return 0

    lax.fori_loop(0, PULSE_OUTER // 2, inner, 0, unroll=4)


def azimuth_forward(got, filt, half):
    g1 = turned_tables(PULSE_OUTER, PULSE_INNER, -1.0)
    re, im = dft_table(PULSE_INNER, -1.0)
    t2 = bf16(np.block([[re, im], [-im, re]]))
    return pl.pallas_call(
        forward_kernel,
        grid=(1,),
        in_specs=[
            whole((DEVICES, ROWS, LANES)),
            whole(g1.shape),
            whole(t2.shape),
            pl.BlockSpec((1, 2, PULSES, LANES), lambda i: (half, 0, 0, 0)),
        ],
        out_specs=whole((PULSES, LANES)),
        out_shape=jax.ShapeDtypeStruct((PULSES, LANES), jnp.bfloat16),
        scratch_shapes=[
            pltpu.VMEM((PULSES, LANES), jnp.float32),
            pltpu.VMEM((PULSES, LANES), jnp.float32),
        ],
        compiler_params=pltpu.CompilerParams(
            dimension_semantics=("arbitrary",), vmem_limit_bytes=40 * MIB
        ),
        cost_estimate=pl.CostEstimate(
            flops=2 * PULSES * LANES * 512, bytes_accessed=12 * MIB, transcendentals=0
        ),
        name="azimuth_forward",
    )(got, g1, t2, filt)


def inverse_kernel(left, right, taps, bands, g1, t2, out, sel, vs, os):
    index = lax.broadcasted_iota(jnp.int32, (2 * LANES, LANES), 0)
    lane = lax.broadcasted_iota(jnp.int32, (2 * LANES, LANES), 1)
    column = jnp.where(index >= LANES, HALF, 0) + (index & (HALF - 1))
    same = ((index >> 6) & 1) == (lane >> 6)
    want = (lane & (HALF - 1)) + bands[0:1, :]
    for j in range(BAND_MAX):
        hit = same & (column == want + j) & (bands[1:2, :] > j)
        sel[:, j * LANES : (j + 1) * LANES] = jnp.where(hit, 1.0, 0.0).astype(jnp.bfloat16)

    size = GROUP * PULSE_INNER

    def group(g, _):
        at = pl.ds(pl.multiple_of(g * size, size), size)
        source = jnp.concatenate([left[at, :], right[at, :]], axis=1)
        total = None
        for j in range(0, BAND_MAX, 2):
            wide = min(2, BAND_MAX - j)
            picked = dot(source, sel[:, j * LANES : (j + wide) * LANES])
            for k in range(wide):
                term = picked[:, k * LANES : (k + 1) * LANES] * taps[at, j + k : j + k + 1]
                total = term if total is None else total + term
        here = total.astype(jnp.bfloat16)
        turned = times_i(total).astype(jnp.bfloat16)
        for k in range(GROUP):
            kb = g * GROUP + k
            rows = slice(k * PULSE_INNER, (k + 1) * PULSE_INNER)
            both = jnp.concatenate([here[rows], turned[rows]], axis=0)
            vs[pl.ds(kb, PULSE_INNER, stride=PULSE_OUTER), :] = dot(g1[kb], both)
        return 0

    lax.fori_loop(0, PULSE_OUTER // GROUP, group, 0)

    def last(i, _):
        sides = []
        for k in range(2):
            at = pl.ds(pl.multiple_of((2 * i + k) * PULSE_OUTER, PULSE_OUTER), PULSE_OUTER)
            v = vs[at, :]
            sides.append(
                jnp.concatenate([v.astype(jnp.bfloat16), times_i(v).astype(jnp.bfloat16)], axis=0)
            )
        y = dot(t2[...], jnp.concatenate(sides, axis=1))
        for k in range(2):
            os[pl.ds(2 * i + k, KEPT_OUTER, stride=PULSE_INNER), :] = y[
                :, k * LANES : (k + 1) * LANES
            ]
        return 0

    lax.fori_loop(0, PULSE_INNER // 2, last, 0, unroll=2)

    def pack(d, _):
        at = pl.ds(pl.multiple_of(d * FRESH_ROWS, STEP), FRESH_ROWS)
        out[d] = os[at, :].astype(jnp.bfloat16)
        return 0

    lax.fori_loop(0, DEVICES, pack, 0, unroll=4)


def azimuth_inverse(left, right, taps, bands):
    g1 = turned_tables(PULSE_INNER, PULSE_OUTER, 1.0)
    re, im = dft_table(PULSE_OUTER, 1.0)
    t2 = bf16(np.concatenate([re[FIRST_OUTER:], im[FIRST_OUTER:]], axis=1))
    return pl.pallas_call(
        inverse_kernel,
        grid=(1,),
        in_specs=[
            whole((PULSES, LANES)),
            whole((PULSES, LANES)),
            whole((PULSES, BAND_MAX)),
            whole((2, LANES)),
            whole(g1.shape),
            whole(t2.shape),
        ],
        out_specs=whole((DEVICES, FRESH_ROWS, LANES)),
        out_shape=jax.ShapeDtypeStruct((DEVICES, FRESH_ROWS, LANES), jnp.bfloat16),
        scratch_shapes=[
            pltpu.VMEM((2 * LANES, BAND_MAX * LANES), jnp.bfloat16),
            pltpu.VMEM((PULSES, LANES), jnp.float32),
            pltpu.VMEM((FRESH_COUNT, LANES), jnp.float32),
        ],
        compiler_params=pltpu.CompilerParams(
            dimension_semantics=("arbitrary",), vmem_limit_bytes=44 * MIB
        ),
        cost_estimate=pl.CostEstimate(
            flops=2 * PULSES * LANES * (256 * BAND_MAX + 512),
            bytes_accessed=12 * MIB,
            transcendentals=0,
        ),
        name="migrate_inverse",
    )(left, right, taps, bands, g1, t2)


def assemble_kernel(first, second, out):
    low = lane_ids(FRESH_ROWS) < HALF

    def one(n1, _):
        a, b = first[n1].astype(jnp.float32), second[n1].astype(jnp.float32)
        at = pl.ds(pl.multiple_of(n1 * LANES, LANES), LANES)
        out[0, :, at] = jnp.where(low, a, roll_half(b)).astype(jnp.bfloat16)
        out[1, :, at] = jnp.where(low, roll_half(a), b).astype(jnp.bfloat16)
        return 0

    lax.fori_loop(0, first.shape[0], one, 0, unroll=4)


def assemble(first, second):
    block = 32
    return pl.pallas_call(
        assemble_kernel,
        grid=(RANGE_OUTER // block,),
        in_specs=[pl.BlockSpec((block, FRESH_ROWS, LANES), lambda i: (i, 0, 0))] * 2,
        out_specs=pl.BlockSpec((2, FRESH_ROWS, block * LANES), lambda i: (0, 0, i)),
        out_shape=jax.ShapeDtypeStruct((2, FRESH_ROWS, RANGE_BINS), jnp.bfloat16),
        compiler_params=pltpu.CompilerParams(
            dimension_semantics=("arbitrary",), vmem_limit_bytes=24 * MIB
        ),
        cost_estimate=pl.CostEstimate(
            flops=4 * FRESH_ROWS * RANGE_BINS, bytes_accessed=6 * MIB, transcendentals=0
        ),
        name="assemble",
    )(first, second)


def exchanged(blocks):
    return lax.all_to_all(blocks, AXES, split_axis=0, concat_axis=0, tiled=True)


def from_next(block):
    size = lax.axis_size(AXES)
    return lax.ppermute(block, AXES, [(i + 1, i) for i in range(size - 1)])


def on_device(
    slab_echoes,
    fresh_pulses,
    range_filter,
    azimuth_filter,
    migration_taps,
    band_offsets,
    band_widths,
):
    packed0, packed1 = range_compress(slab_echoes, fresh_pulses, range_filter)
    filt = filter_by_outer(azimuth_filter)
    taps = migration_taps.reshape(BAND_MAX, PULSE_INNER, PULSE_OUTER)
    taps = taps.transpose(2, 1, 0).reshape(PULSES, BAND_MAX)
    bands = jnp.stack([band_offsets, band_widths]).reshape(2, 2, 1, HALF)
    bands = jnp.broadcast_to(bands, (2, 2, 2, HALF)).reshape(2, 2, LANES)
    spectra0 = azimuth_forward(exchanged(packed0), filt, 0)
    rim = from_next(spectra0)
    spectra1 = azimuth_forward(exchanged(packed1), filt, 1)
    done0 = exchanged(azimuth_inverse(spectra0, spectra1, taps, bands[:, 0]))
    done1 = exchanged(azimuth_inverse(spectra1, rim, taps, bands[:, 1]))
    return assemble(done0, done1)


def solution(mesh):
    placed = (
        P(None, AXES, None),
        P(None, AXES, None),
        P(),
        P(None, None, AXES),
        P(),
        P(AXES),
        P(AXES),
    )
    return jax.shard_map(
        on_device,
        mesh=mesh,
        in_specs=placed,
        out_specs=P(None, AXES, None),
        check_vma=False,
    )
```

time: 459 us -> 259 us (0.56); the launches traced: 451 us -> 258 us
  local copies, waits for them, and re-layouts: 231 us -> 24.7 us
  Pallas kernels: 0 us -> 140 us
  matrix products: 91.3 us -> 0 us
  waiting for transfers between devices: 25.4 us -> 0.01 us
  other arithmetic: 24.8 us -> 0.01 us
  blocking collectives: 52.8 us -> 75.8 us
  starting transfers between devices: 24.7 us -> 17.4 us
    pallas_call x0 -> x7, Pallas kernels: none -> 140 us  [the longest x2 68.5 us: azimuth_inverse(): pl.pallas_call(inverse_kernel, grid=(1,), in_specs=[whole((PULSES, LANES)...]
    dot_general x21 -> x0, matrix products: 91.3 us -> none  [the longest x9 70.5 us: migrate(): jnp.einsum('cpe,en->cpn', extended, selector, preferred_element_type=jnp....]
    unnamed x43 -> x44, local copies, waits for them, and re-layouts: 105 us -> 19.9 us
    convert_element_type x4 -> x0, local copies, waits for them, and re-layouts: 51.2 us -> none  [the longest x2 27.9 us: azimuth_inverse(): return focused.reshape(2, FRESH_COUNT, local_bins).astype(jnp.bfloat16)]
    all_to_all x4 -> x0, local copies, waits for them, and re-layouts: 35.3 us -> none  [the longest x1 16.5 us: on_device(): lax.all_to_all(slab_done, ('az', 'rg'), split_axis=2, concat_axis=1, tile...]
    ppermute x1, waiting for transfers between devices: 25.4 us -> 0.01 us  [from_next(): return lax.ppermute(block, AXES, [(i + 1, i) for i in range(size - 1)])]
    all_to_all x1 -> x2, blocking collectives: 52.8 us -> 75.8 us  [exchanged(): return lax.all_to_all(blocks, AXES, split_axis=0, concat_axis=0, tiled=True)]
    slice x6 -> x0, local copies, waits for them, and re-layouts: 20.1 us -> none  [the longest x2 7.73 us: complex_mul(): values[0] * real_part - values[1] * imag_part]
  transfers between devices with their start and end apart: 3 -> 3, of which waited for: 1 -> 0; matrix products, arithmetic and copies ran while one was open for 25% -> 2% of each run, Pallas kernels for 0% -> 41%
where the time goes in v1:
time: 259 us; the launch traced here: 258 us
  Pallas kernels  140 us (54%)
  blocking collectives  75.8 us (29%)
  local copies, waits for them, and re-layouts  24.7 us (10%)
  starting transfers between devices  17.4 us (7%)
    all_to_all x2, blocking collectives, exchanged(): return lax.all_to_all(blocks, AXES, split_axis=0, concat_axis=0, tiled=True)  75.8 us
    pallas_call x2, Pallas kernels, azimuth_inverse(): pl.pallas_call(inverse_kernel, grid=(1,), in_specs=[whole((PULSES, LANES)...  68.5 us
    pallas_call x2, Pallas kernels, azimuth_forward(): pl.pallas_call(forward_kernel, grid=(1,), in_specs=[whole((DEVICES, ROWS,...  32.4 us
    pallas_call x1, Pallas kernels, range_compress(): pl.pallas_call(range_kernel, grid=(ROWS // STEP,), in_specs=[whole((2, ST...  29.3 us
    unnamed x44, local copies, waits for them, and re-layouts  19.9 us
    all_to_all x2, starting transfers between devices, exchanged(): return lax.all_to_all(blocks, AXES, split_axis=0, concat_axis=0, tiled=True)  14.4 us
    pallas_call x1, Pallas kernels, filter_by_outer(): pl.pallas_call(filter_kernel, grid=(PULSE_OUTER // STEP,), in_specs=[pl.B...  6.11 us
  transfers between devices with their start and end apart: 3, of which 0 were waited for; matrix products, arithmetic and copies ran while one was open for 2% of the time, Pallas kernels for 41%

profile of v1, /device:TPU:1, one launch (start us, length us, event | category | flops | bytes accessed | tf_op | source)
XLA Modules:
  0.0 258.5 jit_solution(11222802658099548064)
XLA Ops:
  0.0 0.9 copy.27
  0.9 0.0 copy-start.9
  0.9 1.9 copy-done.9
  2.8 0.0 copy-start.10
  2.8 1.2 copy-done.10
  4.0 0.0 copy-start.13
  4.0 0.9 copy-done.13
  4.9 0.0 copy-start.14
  4.9 0.9 copy-done.14
  5.8 0.0 copy-start.15
  5.8 0.9 copy-done.15
  6.7 0.0 copy-start.16
  6.8 0.9 copy-done.16
  7.7 29.3 %range_compress.1 = (bf16[128,64,128]{2,1,0:T(8,128)(2,1)S(1)}, bf16[128,64,128]{2,1,0:T(8,128)(2,1)S(1)}) custom-call(bf16[2,16,16384]{2,1,0:T(8,128)(2,1)S(1)} %copy-done.10, bf16[2,48,16384]{2,1,0:T(8,128)(2,1)S(1)} %copy-done.9, f32[2,128,128]{2,1,0:T(8,128)S(1)} %bitcast.20, bf16[256,256]{1,0:T(8,128)(2,1)S(1)} %copy-done.13, ...), custom_call_target="tpu_custom_call" | custom-call | flops 4294967296 | bytes 8388608 | tf_op jit(solution)/shard_map/range_compress/pallas_call | solution.py:206
  37.0 0.0 copy-start.5
  37.0 41.4 %all_to_all.20.got = bf16[128,64,128]{2,1,0:T(8,128)(2,1)} all-to-all(bf16[128,64,128]{2,1,0:T(8,128)(2,1)S(1)} %get-tuple-element.7), channel_id=1, replica_groups=mesh['az'=8,'rg'=16] {'az','rg'}, dimensions={0} | all-to-all | bytes 4194304 | tf_op jit(solution)/shard_map/all_to_all | solution.py:462
  78.4 0.0 copy-done.5
  78.4 4.8 %all-to-all-start.1 = ((bf16[128,64,128]{2,1,0:T(8,128)(2,1)}), bf16[128,64,128]{2,1,0:T(8,128)(2,1)S(1)}, u32[]{:S(2)}, u32[]{:S(2)}) async-start(bf16[128,64,128]{2,1,0:T(8,128)(2,1)} %copy-done.5), calls=%async_computation.1 | async-start | bytes 4194304 | tf_op jit(solution)/shard_map/all_to_all | solution.py:462
  83.2 0.0 copy-start.4
  83.2 2.2 copy-done.4
  85.4 0.0 copy-start.1
  85.4 0.0 copy-start.3
  85.4 0.0 copy-start.8
  85.4 6.1 %filter_by_outer.1.filt = bf16[2,2,8192,128]{3,2,1,0:T(8,128)(2,1)S(1)} custom-call(bf16[2,64,128,128]{3,2,1,0:T(8,128)(2,1)S(1)} %bitcast.19), custom_call_target="tpu_custom_call" | custom-call | flops 8388608 | bytes 12582912 | tf_op jit(solution)/shard_map/filter_by_outer/pallas_call | solution.py:253
  91.5 0.0 copy-start
  91.5 3.3 %copy-done = bf16[2,2,8192,128]{3,2,1,0:T(8,128)(2,1)} copy-done((bf16[2,2,8192,128]{3,2,1,0:T(8,128)(2,1)}, bf16[2,2,8192,128]{3,2,1,0:T(8,128)(2,1)S(1)}, u32[]{:S(2)}) %copy-start) | copy-done | bytes 8388632
  94.8 0.0 copy-done.1
  94.8 0.0 copy-done.3
  94.8 0.0 copy-done.8
  94.8 0.0 copy-start.18
  94.8 16.8 %azimuth_forward.2.left = bf16[8192,128]{1,0:T(8,128)(2,1)} custom-call(bf16[128,64,128]{2,1,0:T(8,128)(2,1)S(1)} %copy-done.3, bf16[64,128,256]{2,1,0:T(8,128)(2,1)S(1)} %copy-done.1, bf16[128,128]{1,0:T(8,128)(2,1)S(1)} %copy-done.8, bf16[2,2,8192,128]{3,2,1,0:T(8,128)(2,1)} %copy-done), custom_call_target="tpu_custom_call" | custom-call | flops 1073741824 | bytes 12582912 | tf_op jit(solution)/shard_map/azimuth_forward/pallas_call | solution.py:313
  111.6 3.0 %collective-permute-start = (bf16[8192,128]{1,0:T(8,128)(2,1)}, bf16[8192,128]{1,0:T(8,128)(2,1)}, u32[]{:S(2)}, u32[]{:S(2)}) collective-permute-start(bf16[8192,128]{1,0:T(8,128)(2,1)} %azimuth_forward.2.left), channel_id=1, source_target_pairs={{1,0},{2,1},{3,2},{4,3},{5,4},{6,5},{7,6},{8,7},{9,8},{10,9},{11,1... | collective-permute-start | bytes 6291464 | tf_op jit(solution)/shard_map/ppermute | solution.py:467
  114.6 0.0 copy-done.18
  114.6 0.1 copy.25
  114.7 0.0 copy-start.19
  114.7 0.0 copy-start.20
  114.8 4.5 %copy.22 = f32[9,64,128]{0,1,2:T(8,128)} copy(f32[9,64,128]{2,1,0:T(8,128)S(1)} %slice.10) | data formatting | bytes 589824 | tf_op jit(solution)/shard_map/reshape | solution.py:481
  119.3 0.0 copy-done.19
  119.3 0.1 stack.10
  119.3 0.0 copy-done.20
  119.3 0.1 stack.9
  119.4 0.1 reshape.24
  119.5 0.0 all-to-all-done.1.got
  119.5 0.0 copy-start.2
  119.5 2.2 copy-done.2
  121.7 0.0 copy-start.11
  121.7 0.0 copy-start.17
  121.7 15.6 %azimuth_forward.3.right.left = bf16[8192,128]{1,0:T(8,128)(2,1)S(1)} custom-call(bf16[128,64,128]{2,1,0:T(8,128)(2,1)S(1)} %all-to-all-done.1.got, bf16[64,128,256]{2,1,0:T(8,128)(2,1)S(1)} %copy-done.2, bf16[128,128]{1,0:T(8,128)(2,1)S(1)} %copy-done.8, bf16[2,2,8192,128]{3,2,1,0:T(8,128)(2,1)} %copy-done), custom_call_target="tpu_custom_call" | custom-call | flops 1073741824 | bytes 12582912 | tf_op jit(solution)/shard_map/azimuth_forward/pallas_call | solution.py:313
  137.3 0.0 copy-done.11
  137.3 0.0 copy-done.17
  137.3 34.9 %migrate_inverse.2 = bf16[128,48,128]{2,1,0:T(8,128)(2,1)} custom-call(bf16[8192,128]{1,0:T(8,128)(2,1)} %azimuth_forward.2.left, bf16[8192,128]{1,0:T(8,128)(2,1)S(1)} %azimuth_forward.3.right.left, f32[8192,9]{1,0:T(8,128)} %bitcast.21, s32[2,128]{1,0:T(2,128)S(1)} %get-tuple-element.10.bands, bf16[128,64,128]{2,1,0:T(8,128)(2,1)S(1)} %copy-done.11, ...), custom_call_target="tpu_custom_call" | custom-call | flops 5905580032 | bytes 12582912 | tf_op jit(solution)/shard_map/migrate_inverse/pallas_call | solution.py:400
  172.2 0.0 copy-start.6
  172.2 1.3 copy-done.6
  173.5 9.6 %all-to-all-start.2 = ((bf16[128,48,128]{2,1,0:T(8,128)(2,1)}), bf16[128,48,128]{2,1,0:T(8,128)(2,1)S(1)}, u32[]{:S(2)}, u32[]{:S(2)}) async-start(bf16[128,48,128]{2,1,0:T(8,128)(2,1)} %migrate_inverse.2), calls=%async_computation.2 | async-start | bytes 3145728 | tf_op jit(solution)/shard_map/all_to_all | solution.py:462
  183.1 0.0 collective-permute-done.right
  183.1 0.0 copy-start.7
  183.1 1.6 copy-done.7
  184.7 0.0 copy-start.12
  184.7 1.6 copy-done.12
  186.3 33.7 %migrate_inverse.3 = bf16[128,48,128]{2,1,0:T(8,128)(2,1)S(1)} custom-call(bf16[8192,128]{1,0:T(8,128)(2,1)S(1)} %copy-done.7, bf16[8192,128]{1,0:T(8,128)(2,1)} %collective-permute-done.right, f32[8192,9]{1,0:T(8,128)} %bitcast.22, s32[2,128]{1,0:T(2,128)S(1)} %get-tuple-element.9.bands, bf16[128,64,128]{2,1,0:T(8,128)(2,1)S(1)} %copy-done.12, ...), custom_call_target="tpu_custom_call" | custom-call | flops 5905580032 | bytes 12582912 | tf_op jit(solution)/shard_map/migrate_inverse/pallas_call | solution.py:400
  220.0 0.0 all-to-all-done.2.first
  220.0 34.3 %all_to_all.21.second = bf16[128,48,128]{2,1,0:T(8,128)(2,1)S(1)} all-to-all(bf16[128,48,128]{2,1,0:T(8,128)(2,1)S(1)} %migrate_inverse.3), channel_id=1, replica_groups=mesh['az'=8,'rg'=16] {'az','rg'}, dimensions={0} | all-to-all | bytes 3145728 | tf_op jit(solution)/shard_map/all_to_all | solution.py:462
  254.3 4.2 %assemble.1 = bf16[2,48,16384]{2,1,0:T(8,128)(2,1)} custom-call(bf16[128,48,128]{2,1,0:T(8,128)(2,1)S(1)} %all-to-all-done.2.first, bf16[128,48,128]{2,1,0:T(8,128)(2,1)S(1)} %all_to_all.21.second), custom_call_target="tpu_custom_call" | custom-call | flops 3145728 | bytes 6291456 | tf_op jit(solution)/shard_map/assemble/pallas_call | solution.py:445
  (5 shorter events, 0.0 us)
Async XLA Ops:
  0.9 1.9 copy-start.9
  2.8 1.2 copy-start.10
  4.0 0.9 copy-start.13
  4.9 0.9 copy-start.14
  5.8 0.9 copy-start.15
  6.7 0.9 copy-start.16
  37.0 41.4 %copy-start.5 = (bf16[128,64,128]{2,1,0:T(8,128)(2,1)}, bf16[128,64,128]{2,1,0:T(8,128)(2,1)S(1)}, u32[]{:S(2)}) copy-start(bf16[128,64,128]{2,1,0:T(8,128)(2,1)S(1)} %get-tuple-element.8) | copy-start | bytes 6291460
  78.4 41.1 %all-to-all-start.1 = ((bf16[128,64,128]{2,1,0:T(8,128)(2,1)}), bf16[128,64,128]{2,1,0:T(8,128)(2,1)S(1)}, u32[]{:S(2)}, u32[]{:S(2)}) async-start(bf16[128,64,128]{2,1,0:T(8,128)(2,1)} %copy-done.5), calls=%async_computation.1 | async-start | bytes 4194304 | tf_op jit(solution)/shard_map/all_to_all | solution.py:462
  83.2 2.2 copy-start.4
  85.4 9.4 %copy-start.1 = (bf16[64,128,256]{2,1,0:T(8,128)(2,1)S(1)}, bf16[64,128,256]{2,1,0:T(8,128)(2,1)}, u32[]{:S(2)}) copy-start(bf16[64,128,256]{2,1,0:T(8,128)(2,1)} %constant.20.clone.g1) | copy-start | bytes 12582916
  85.4 9.4 %copy-start.3 = (bf16[128,64,128]{2,1,0:T(8,128)(2,1)S(1)}, bf16[128,64,128]{2,1,0:T(8,128)(2,1)}, u32[]{:S(2)}) copy-start(bf16[128,64,128]{2,1,0:T(8,128)(2,1)} %all_to_all.20.got) | copy-start | bytes 6291460
  85.4 9.4 %copy-start.8 = (bf16[128,128]{1,0:T(8,128)(2,1)S(1)}, bf16[128,128]{1,0:T(8,128)(2,1)}, u32[]{:S(2)}) copy-start(bf16[128,128]{1,0:T(8,128)(2,1)} %constant.21.clone.t2) | copy-start | bytes 98308
  91.5 3.3 %copy-start = (bf16[2,2,8192,128]{3,2,1,0:T(8,128)(2,1)}, bf16[2,2,8192,128]{3,2,1,0:T(8,128)(2,1)S(1)}, u32[]{:S(2)}) copy-start(bf16[2,2,8192,128]{3,2,1,0:T(8,128)(2,1)S(1)} %filter_by_outer.1.filt) | copy-start | bytes 25165828
  94.8 19.8 %copy-start.18 = (f32[9,8192]{1,0:T(8,128)S(1)}, f32[9,8192]{1,0:T(8,128)}, u32[]{:S(2)}) copy-start(f32[9,8192]{1,0:T(8,128)} %param.25) | copy-start | bytes 884740
  111.6 71.5 %collective-permute-start = (bf16[8192,128]{1,0:T(8,128)(2,1)}, bf16[8192,128]{1,0:T(8,128)(2,1)}, u32[]{:S(2)}, u32[]{:S(2)}) collective-permute-start(bf16[8192,128]{1,0:T(8,128)(2,1)} %azimuth_forward.2.left), channel_id=1, source_target_pairs={{1,0},{2,1},{3,2},{4,3},{5,4},{6,5},{7,6},{8,7},{9,8},{10,9},{11,1... | collective-permute-start | bytes 6291464 | tf_op jit(solution)/shard_map/ppermute | solution.py:467
  114.7 4.5 %copy-start.19 = (s32[128]{0:T(128)S(1)}, s32[128]{0:T(128)}, u32[]{:S(2)}) copy-start(s32[128]{0:T(128)} %param.27) | copy-start | bytes 1540
  114.7 4.6 %copy-start.20 = (s32[128]{0:T(128)S(1)}, s32[128]{0:T(128)}, u32[]{:S(2)}) copy-start(s32[128]{0:T(128)} %param.26) | copy-start | bytes 1540
  119.5 2.2 copy-start.2
  121.7 15.6 %copy-start.11 = (bf16[128,64,128]{2,1,0:T(8,128)(2,1)S(1)}, bf16[128,64,128]{2,1,0:T(8,128)(2,1)}, u32[]{:S(2)}) copy-start(bf16[128,64,128]{2,1,0:T(8,128)(2,1)} %constant.22.clone.g1) | copy-start | bytes 6291460
  121.7 15.6 %copy-start.17 = (bf16[96,256]{1,0:T(8,128)(2,1)S(1)}, bf16[96,256]{1,0:T(8,128)(2,1)}, u32[]{:S(2)}) copy-start(bf16[96,256]{1,0:T(8,128)(2,1)} %constant.23.clone.t2) | copy-start | bytes 147460
  172.2 1.3 copy-start.6
  173.5 46.5 %all-to-all-start.2 = ((bf16[128,48,128]{2,1,0:T(8,128)(2,1)}), bf16[128,48,128]{2,1,0:T(8,128)(2,1)S(1)}, u32[]{:S(2)}, u32[]{:S(2)}) async-start(bf16[128,48,128]{2,1,0:T(8,128)(2,1)} %migrate_inverse.2), calls=%async_computation.2 | async-start | bytes 3145728 | tf_op jit(solution)/shard_map/all_to_all | solution.py:462
  183.1 1.6 copy-start.7
  184.7 1.6 copy-start.12

commit v2 on v1

v2 whole, which is shorter than its diff:
```python
import functools
import math

import jax
import jax.numpy as jnp
import ml_dtypes
import numpy as np
from jax import lax
from jax.experimental import pallas as pl
from jax.experimental.pallas import tpu as pltpu
from jax.sharding import PartitionSpec as P

RANGE_OUTER = 128
RANGE_INNER = 128
PULSE_OUTER = 128
PULSE_INNER = 64
SLAB_PULSES = 2048
BAND_MAX = 9
RANGE_BINS = 16384
PULSES = 8192
FRESH_COUNT = 6144
LANES = 128
HALF = 64
DEVICES = 128
SLAB_ROWS = SLAB_PULSES // DEVICES
FRESH_ROWS = FRESH_COUNT // DEVICES
ROWS = SLAB_ROWS + FRESH_ROWS
STEP = 16
FIRST_OUTER = SLAB_PULSES // PULSE_INNER
KEPT_OUTER = PULSE_OUTER - FIRST_OUTER
GROUP = 4
UNROLL = 8
PITCH = STEP + 8
INNER_PITCH = PULSE_INNER + 8
OUTER_PITCH = PULSE_OUTER + 8
BLOCKS = ROWS // STEP
RANGE_LIMIT = 60
FWD_LIMIT = 60
INV_LIMIT = 60
PARTS = 4
ASSEMBLE = 32
AXES = ("az", "rg")
MIB = 1024 * 1024


def bf16(values):
    return np.asarray(values, np.float32).astype(ml_dtypes.bfloat16)


def dft_table(length, sign):
    index = np.arange(length)
    angle = (np.outer(index, index) % length).astype(np.float32) * np.float32(
        2.0 * math.pi / length
    )
    scale = np.float32(1.0 / math.sqrt(length))
    real_part = bf16(np.cos(angle) * scale).astype(np.float32)
    imag_part = bf16(sign * np.sin(angle) * scale).astype(np.float32)
    return real_part, imag_part


def twiddle(rows_size, cols_size, total, sign):
    angle = (np.outer(np.arange(rows_size), np.arange(cols_size)) % total).astype(
        np.float32
    ) * np.float32(2.0 * math.pi / total)
    return np.cos(angle), np.float32(sign) * np.sin(angle)


def left_table(length, sign):
    re, im = dft_table(length, sign)
    return bf16(np.block([[re, -im], [im, re]]))


def right_table(length, sign):
    re, im = dft_table(length, sign)
    return bf16(np.block([[re, im], [-im, re]]))


def turned_tables(outer, inner, sign):
    re, im = dft_table(outer, sign)
    tw_re, tw_im = twiddle(outer, inner, PULSES, sign)
    turn_re, turn_im = tw_re.T[:, :, None], tw_im.T[:, :, None]
    return bf16(
        np.concatenate(
            [re * turn_re - im * turn_im, re * turn_im + im * turn_re], axis=2
        )
    )


def turn_table():
    one = np.eye(HALF, dtype=np.float32)
    return bf16(np.block([[0 * one, one], [-one, 0 * one]]))


def roll_half(values):
    return pltpu.roll(values, HALF, 1)


def lane_ids(rows):
    return lax.broadcasted_iota(jnp.int32, (rows, LANES), 1)


def times_i(values):
    turned = roll_half(values)
    return jnp.where(lane_ids(values.shape[0]) < HALF, -turned, turned)


def dot(left, right):
    return jnp.dot(left, right, preferred_element_type=jnp.float32)


def in_vmem():
    return pl.BlockSpec(memory_space=pltpu.VMEM)


def in_hbm():
    return pl.BlockSpec(memory_space=pl.ANY)


def range_kernel(slab, fresh, filt, t1, t2, t3, t4, w_in, w_out, out, xs, os, hs, first, second, third):
    step = pl.program_id(0)

    def load(source):
        def one(n1, _):
            at = pl.ds(pl.multiple_of(n1 * LANES, LANES), LANES)
            to = pl.ds(pl.multiple_of(n1 * PITCH, 8), STEP)
            for c in range(2):
                xs[c, to, :] = source[c, :, at].astype(jnp.float32)
            return 0

        lax.fori_loop(0, RANGE_OUTER, one, 0, unroll=8)

    @pl.when(step == 0)
    def _():
        for c in range(2):
            for k2 in range(RANGE_INNER):
                hs[2 + c, k2 : k2 + 1, :] = filt[c : c + 1, k2 * LANES : (k2 + 1) * LANES]
            hs[c] = hs[2 + c].T
        load(slab)

    @pl.when(step > 0)
    def _():
        load(fresh)

    def rows(p):
        return pl.ds(p, RANGE_OUTER, stride=PITCH)

    def stage1(i, _):
        ps = (2 * i, 2 * i + 1)
        x = jnp.concatenate(
            [
                jnp.concatenate([xs[c, rows(p), :].astype(jnp.bfloat16) for p in ps], axis=1)
                for c in range(2)
            ],
            axis=0,
        )
        y = dot(t1[...], x)
        for k in range(2):
            re, im = y[:LANES, k * LANES : (k + 1) * LANES], y[LANES:, k * LANES : (k + 1) * LANES]
            at = pl.ds(pl.multiple_of((2 * i + k) * LANES, LANES), LANES)
            first[at, :LANES] = (re * w_in[0] - im * w_in[1]).astype(jnp.bfloat16)
            first[at, LANES:] = (re * w_in[1] + im * w_in[0]).astype(jnp.bfloat16)
        return 0

    def stage2(i, _):
        at = pl.ds(pl.multiple_of(2 * i * LANES, 2 * LANES), 2 * LANES)
        y = dot(first[at, :], t2[...])
        for k in range(2):
            re, im = y[k * LANES : (k + 1) * LANES, :LANES], y[k * LANES : (k + 1) * LANES, LANES:]
            at = pl.ds(pl.multiple_of((2 * i + k) * LANES, LANES), LANES)
            second[at, :LANES] = (re * hs[0] - im * hs[1]).astype(jnp.bfloat16)
            second[at, LANES:] = (re * hs[1] + im * hs[0]).astype(jnp.bfloat16)
        return 0

    def stage3(i, _):
        at = pl.ds(pl.multiple_of(2 * i * LANES, 2 * LANES), 2 * LANES)
        y = dot(second[at, :], t3[...])
        for k in range(2):
            re, im = y[k * LANES : (k + 1) * LANES, :LANES], y[k * LANES : (k + 1) * LANES, LANES:]
            cols = slice(k * LANES, (k + 1) * LANES)
            third[i, :LANES, cols] = (re * w_out[0] - im * w_out[1]).astype(jnp.bfloat16)
            third[i, LANES:, cols] = (re * w_out[1] + im * w_out[0]).astype(jnp.bfloat16)
        return 0

    def stage4(i, _):
        y = dot(t4[...], third[i])
        low = lane_ids(LANES) < HALF
        for k in range(2):
            p = 2 * i + k
            re, im = y[:LANES, k * LANES : (k + 1) * LANES], y[LANES:, k * LANES : (k + 1) * LANES]
            os[0, rows(p), :] = jnp.where(low, re, roll_half(im))
            os[1, rows(p), :] = jnp.where(low, roll_half(re), im)
        return 0

    for stage in (stage1, stage2, stage3, stage4):
        lax.fori_loop(0, STEP // 2, stage, 0, unroll=UNROLL)

    def store(n1, _):
        at = pl.ds(pl.multiple_of(n1 * PITCH, 8), STEP)
        out[n1, 0] = os[0, at, :].astype(jnp.bfloat16)
        out[n1, 1] = os[1, at, :].astype(jnp.bfloat16)
        return 0

    lax.fori_loop(0, RANGE_OUTER, store, 0, unroll=8)


def whole(shape):
    return pl.BlockSpec(shape, lambda *_: (0,) * len(shape))


def range_compress(slab, fresh, range_filter):
    tables = (
        left_table(RANGE_OUTER, -1.0),
        right_table(RANGE_INNER, -1.0),
        right_table(RANGE_INNER, 1.0),
        left_table(RANGE_OUTER, 1.0),
    )
    w_in = np.stack(twiddle(RANGE_OUTER, RANGE_INNER, RANGE_BINS, -1.0))
    w_out = np.stack(twiddle(RANGE_OUTER, RANGE_INNER, RANGE_BINS, 1.0))
    square = whole((2 * LANES, 2 * LANES))
    part = whole((2, LANES, LANES))
    out = jax.ShapeDtypeStruct((DEVICES, 2, ROWS, LANES), jnp.bfloat16)
    return pl.pallas_call(
        range_kernel,
        grid=(ROWS // STEP,),
        in_specs=[
            whole((2, STEP, RANGE_BINS)),
            pl.BlockSpec((2, STEP, RANGE_BINS), lambda i: (0, jnp.maximum(i - 1, 0), 0)),
            whole((2, RANGE_BINS)),
            square,
            square,
            square,
            square,
            part,
            part,
        ],
        out_specs=pl.BlockSpec((DEVICES, 2, STEP, LANES), lambda i: (0, 0, i, 0)),
        out_shape=out,
        scratch_shapes=[
            pltpu.VMEM((2, RANGE_OUTER * PITCH, LANES), jnp.float32),
            pltpu.VMEM((2, RANGE_OUTER * PITCH, LANES), jnp.float32),
            pltpu.VMEM((4, LANES, LANES), jnp.float32),
            pltpu.VMEM((STEP * LANES, 2 * LANES), jnp.bfloat16),
            pltpu.VMEM((STEP * LANES, 2 * LANES), jnp.bfloat16),
            pltpu.VMEM((STEP // 2, 2 * LANES, 2 * LANES), jnp.bfloat16),
        ],
        compiler_params=pltpu.CompilerParams(
            dimension_semantics=("arbitrary",), vmem_limit_bytes=RANGE_LIMIT * MIB
        ),
        cost_estimate=pl.CostEstimate(
            flops=4 * 2 * ROWS * RANGE_BINS * 512, bytes_accessed=8 * MIB, transcendentals=0
        ),
        name="range_compress",
    )(slab, fresh, range_filter, *tables, w_in, w_out)


def prepare_kernel(filt, taps, out, wide, fs):
    for c in range(2):
        for kl in range(PULSE_INNER):
            fs[c, kl * PITCH : kl * PITCH + STEP, :] = filt[c, kl].astype(jnp.float32)
    low = lane_ids(PULSE_INNER) < HALF
    for kb in range(STEP):
        for c in range(2):
            value = fs[c, pl.ds(kb, PULSE_INNER, stride=PITCH), :]
            turned = roll_half(value)
            at = slice(kb * PULSE_INNER, (kb + 1) * PULSE_INNER)
            out[0, c, at, :] = jnp.where(low, value, turned).astype(jnp.bfloat16)
            out[1, c, at, :] = jnp.where(low, turned, value).astype(jnp.bfloat16)

    def spread(i, _):
        at = pl.ds(pl.multiple_of(i * STEP, STEP), STEP)
        for j in range(BAND_MAX):
            column = jnp.broadcast_to(taps[at, j : j + 1], (STEP, LANES))
            wide[j, at, :] = column.astype(jnp.bfloat16)
        return 0

    lax.fori_loop(0, PULSE_INNER, spread, 0, unroll=4)


def prepare(azimuth_filter, taps):
    folded = azimuth_filter.reshape(2, PULSE_INNER, PULSE_OUTER, LANES)
    rows = STEP * PULSE_INNER
    return pl.pallas_call(
        prepare_kernel,
        grid=(PULSE_OUTER // STEP,),
        in_specs=[
            pl.BlockSpec((2, PULSE_INNER, STEP, LANES), lambda i: (0, 0, i, 0)),
            pl.BlockSpec((rows, BAND_MAX), lambda i: (i, 0)),
        ],
        out_specs=[
            pl.BlockSpec((2, 2, rows, LANES), lambda i: (0, 0, i, 0)),
            pl.BlockSpec((BAND_MAX, rows, LANES), lambda i: (0, i, 0)),
        ],
        out_shape=[
            jax.ShapeDtypeStruct((2, 2, PULSES, LANES), jnp.bfloat16),
            jax.ShapeDtypeStruct((BAND_MAX, PULSES, LANES), jnp.bfloat16),
        ],
        scratch_shapes=[pltpu.VMEM((2, PULSE_INNER * PITCH, LANES), jnp.float32)],
        compiler_params=pltpu.CompilerParams(
            dimension_semantics=("arbitrary",), vmem_limit_bytes=60 * MIB
        ),
        cost_estimate=pl.CostEstimate(
            flops=8 * PULSES * LANES, bytes_accessed=34 * MIB, transcendentals=0
        ),
        name="prepare",
    )(folded, taps)


def start_all(pairs, sems):
    copies = [pltpu.make_async_copy(a, b, sems.at[i]) for i, (a, b) in enumerate(pairs)]
    for copy in copies:
        copy.start()
    return copies


def forward_kernel(
    half, got_hbm, g1_hbm, t2, filt_hbm, out_hbm, got, g1, filt, out, ps, ts, sems, out_sems
):
    get_got, get_g1, get_filt = start_all(
        ((got_hbm.at[:, half], got), (g1_hbm, g1), (filt_hbm.at[half], filt)), sems
    )
    get_got.wait()
    quarter = PULSE_INNER // STEP
    fresh_units = FRESH_ROWS // STEP

    def unpack(g, _):
        slab = pl.multiple_of(g * INNER_PITCH, 8)
        base = pl.multiple_of((FIRST_OUTER + g * fresh_units) * INNER_PITCH, 8)
        for d in range(quarter):
            block = got[g * quarter + d].astype(jnp.float32)
            ps[pl.ds(slab + d * STEP, STEP), :] = block[:STEP]
            for k in range(fresh_units):
                unit = d * fresh_units + k
                at = base + (unit // quarter) * INNER_PITCH + (unit % quarter) * STEP
                ps[pl.ds(at, STEP), :] = block[(k + 1) * STEP : (k + 2) * STEP]
        return 0

    lax.fori_loop(0, DEVICES // quarter, unpack, 0, unroll=2)

    def outer(l, _):
        x = ps[pl.ds(l, PULSE_OUTER, stride=INNER_PITCH), :]
        both = jnp.concatenate([x.astype(jnp.bfloat16), times_i(x).astype(jnp.bfloat16)], axis=0)
        ts[pl.ds(l, PULSE_OUTER, stride=INNER_PITCH), :] = dot(g1[l], both)
        return 0

    get_g1.wait()
    lax.fori_loop(0, PULSE_INNER, outer, 0, unroll=16)

    def inner(i, _):
        sides = []
        for k in range(2):
            at = pl.ds(pl.multiple_of((2 * i + k) * INNER_PITCH, 8), PULSE_INNER)
            t = ts[at, :]
            sides.append(
                jnp.concatenate([t.astype(jnp.bfloat16), times_i(t).astype(jnp.bfloat16)], axis=0)
            )
        y = dot(t2[...], jnp.concatenate(sides, axis=1))
        for k in range(2):
            at = pl.ds(pl.multiple_of((2 * i + k) * PULSE_INNER, PULSE_INNER), PULSE_INNER)
            cols = slice(k * LANES, (k + 1) * LANES)
            out[at, :] = (
                y[:PULSE_INNER, cols] * filt[0, at, :].astype(jnp.float32)
                + y[PULSE_INNER:, cols] * filt[1, at, :].astype(jnp.float32)
            ).astype(jnp.bfloat16)
        return 0

    get_filt.wait()
    put_in_parts(inner, PULSE_OUTER // 2, 16, out, out_hbm, out_sems)


def put_in_parts(step, count, unroll, source, target, sems):
    rows = source.shape[0] // PARTS
    copies = []
    for i in range(PARTS):
        lax.fori_loop(i * count // PARTS, (i + 1) * count // PARTS, step, 0, unroll=unroll)
        at = pl.ds(i * rows, rows)
        copies.append(pltpu.make_async_copy(source.at[at], target.at[at], sems.at[i]))
        copies[i].start()
    for copy in copies:
        copy.wait()


def azimuth_forward(got, filt, half):
    g1 = turned_tables(PULSE_OUTER, PULSE_INNER, -1.0)
    re, im = dft_table(PULSE_INNER, -1.0)
    t2 = bf16(np.block([[re, im], [-im, re]]))
    return pl.pallas_call(
        functools.partial(forward_kernel, half),
        in_specs=[in_hbm(), in_hbm(), in_vmem(), in_hbm()],
        out_specs=in_hbm(),
        out_shape=jax.ShapeDtypeStruct((PULSES, LANES), jnp.bfloat16),
        scratch_shapes=[
            pltpu.VMEM((DEVICES, ROWS, LANES), jnp.bfloat16),
            pltpu.VMEM(g1.shape, jnp.bfloat16),
            pltpu.VMEM((2, PULSES, LANES), jnp.bfloat16),
            pltpu.VMEM((PULSES, LANES), jnp.bfloat16),
            pltpu.VMEM((PULSE_OUTER * INNER_PITCH, LANES), jnp.float32),
            pltpu.VMEM((PULSE_OUTER * INNER_PITCH, LANES), jnp.float32),
            pltpu.SemaphoreType.DMA((3,)),
            pltpu.SemaphoreType.DMA((PARTS,)),
        ],
        compiler_params=pltpu.CompilerParams(vmem_limit_bytes=FWD_LIMIT * MIB),
        cost_estimate=pl.CostEstimate(
            flops=2 * PULSES * LANES * 512, bytes_accessed=12 * MIB, transcendentals=0
        ),
        name="azimuth_forward",
    )(got, g1, t2, filt)


def inverse_kernel(
    left_hbm,
    right_hbm,
    taps_hbm,
    bands,
    g1_hbm,
    t2,
    by_i,
    out_hbm,
    left,
    right,
    taps,
    g1,
    out,
    sel,
    sums,
    moved,
    vs,
    os,
    sems,
    out_sems,
):
    starts = range(0, BAND_MAX, 2)
    pairs = [(left_hbm, left), (right_hbm, right)]
    for j in starts:
        at = pl.ds(j, min(2, BAND_MAX - j))
        pairs.append((taps_hbm.at[at], taps.at[at]))
    copies = start_all([*pairs, (g1_hbm, g1)], sems)

    index = lax.broadcasted_iota(jnp.int32, (2 * LANES, LANES), 0)
    lane = lax.broadcasted_iota(jnp.int32, (2 * LANES, LANES), 1)
    column = jnp.where(index >= LANES, HALF, 0) + (index & (HALF - 1))
    same = ((index >> 6) & 1) == (lane >> 6)
    want = (lane & (HALF - 1)) + bands[0:1, :]
    for j in range(BAND_MAX):
        hit = same & (column == want + j) & (bands[1:2, :] > j)
        sel[:, j * LANES : (j + 1) * LANES] = jnp.where(hit, 1.0, 0.0).astype(jnp.bfloat16)

    size = GROUP * PULSE_INNER

    def pick(j, g, _):
        at = pl.ds(pl.multiple_of(g * size, size), size)
        wide = min(2, BAND_MAX - j)
        source = jnp.concatenate([left[at, :], right[at, :]], axis=1)
        picked = dot(source, sel[:, j * LANES : (j + wide) * LANES])
        total = None if j == 0 else sums[at, :]
        for k in range(wide):
            weight = taps[j + k, at, :].astype(jnp.float32)
            term = picked[:, k * LANES : (k + 1) * LANES] * weight
            total = term if total is None else total + term
        if j + wide < BAND_MAX:
            sums[at, :] = total
            return 0
        here = total.astype(jnp.bfloat16)
        for k in range(GROUP):
            moved[g * GROUP + k, :PULSE_INNER, :] = here[k * PULSE_INNER : (k + 1) * PULSE_INNER]
        return 0

    def turn(g, _):
        here = [moved[g * GROUP + k, :PULSE_INNER, :] for k in range(GROUP)]
        turned = dot(jnp.concatenate(here, axis=0), by_i[...]).astype(jnp.bfloat16)
        for k in range(GROUP):
            moved[g * GROUP + k, PULSE_INNER:, :] = turned[k * PULSE_INNER : (k + 1) * PULSE_INNER]
        return 0

    copies[0].wait()
    copies[1].wait()
    for j in starts:
        copies[2 + j // 2].wait()
        lax.fori_loop(0, PULSE_OUTER // GROUP, functools.partial(pick, j), 0, unroll=16)
    lax.fori_loop(0, PULSE_OUTER // GROUP, turn, 0, unroll=8)

    def inner(kb, _):
        vs[pl.ds(kb, PULSE_INNER, stride=OUTER_PITCH), :] = dot(g1[kb], moved[kb])
        return 0

    copies[-1].wait()
    lax.fori_loop(0, PULSE_OUTER, inner, 0, unroll=16)

    def last(i, _):
        sides = []
        for k in range(2):
            at = pl.ds(pl.multiple_of((2 * i + k) * OUTER_PITCH, 8), PULSE_OUTER)
            v = vs[at, :]
            sides.append(
                jnp.concatenate([v.astype(jnp.bfloat16), times_i(v).astype(jnp.bfloat16)], axis=0)
            )
        y = dot(t2[...], jnp.concatenate(sides, axis=1))
        for k in range(2):
            os[pl.ds(2 * i + k, KEPT_OUTER, stride=INNER_PITCH), :] = y[
                :, k * LANES : (k + 1) * LANES
            ]
        return 0

    lax.fori_loop(0, PULSE_INNER // 2, last, 0, unroll=8)

    quarter = PULSE_INNER // STEP
    fresh_units = FRESH_ROWS // STEP

    def pack(g, _):
        base = pl.multiple_of(g * fresh_units * INNER_PITCH, 8)
        for d in range(quarter):
            for k in range(fresh_units):
                unit = d * fresh_units + k
                at = (unit // quarter) * INNER_PITCH + (unit % quarter) * STEP
                out[g * quarter + d, k * STEP : (k + 1) * STEP, :] = os[
                    pl.ds(base + at, STEP), :
                ].astype(jnp.bfloat16)
        return 0

    put_in_parts(pack, DEVICES // quarter, 4, out, out_hbm, out_sems)


def azimuth_inverse(left, right, taps, bands):
    g1 = turned_tables(PULSE_INNER, PULSE_OUTER, 1.0)
    re, im = dft_table(PULSE_OUTER, 1.0)
    t2 = bf16(np.concatenate([re[FIRST_OUTER:], im[FIRST_OUTER:]], axis=1))
    return pl.pallas_call(
        inverse_kernel,
        in_specs=[in_hbm()] * 3 + [in_vmem(), in_hbm(), in_vmem(), in_vmem()],
        out_specs=in_hbm(),
        out_shape=jax.ShapeDtypeStruct((DEVICES, FRESH_ROWS, LANES), jnp.bfloat16),
        scratch_shapes=[
            pltpu.VMEM((PULSES, LANES), jnp.bfloat16),
            pltpu.VMEM((PULSES, LANES), jnp.bfloat16),
            pltpu.VMEM((BAND_MAX, PULSES, LANES), jnp.bfloat16),
            pltpu.VMEM(g1.shape, jnp.bfloat16),
            pltpu.VMEM((DEVICES, FRESH_ROWS, LANES), jnp.bfloat16),
            pltpu.VMEM((2 * LANES, BAND_MAX * LANES), jnp.bfloat16),
            pltpu.VMEM((PULSES, LANES), jnp.float32),
            pltpu.VMEM((PULSE_OUTER, 2 * PULSE_INNER, LANES), jnp.bfloat16),
            pltpu.VMEM((PULSE_INNER * OUTER_PITCH, LANES), jnp.float32),
            pltpu.VMEM((KEPT_OUTER * INNER_PITCH, LANES), jnp.float32),
            pltpu.SemaphoreType.DMA((3 + (BAND_MAX + 1) // 2,)),
            pltpu.SemaphoreType.DMA((PARTS,)),
        ],
        compiler_params=pltpu.CompilerParams(vmem_limit_bytes=INV_LIMIT * MIB),
        cost_estimate=pl.CostEstimate(
            flops=2 * PULSES * LANES * (256 * BAND_MAX + 512),
            bytes_accessed=12 * MIB,
            transcendentals=0,
        ),
        name="migrate_inverse",
    )(left, right, taps, bands, g1, t2, turn_table())


def assemble_kernel(first, second, out):
    low = lane_ids(FRESH_ROWS) < HALF

    def one(n1, _):
        a, b = first[n1].astype(jnp.float32), second[n1].astype(jnp.float32)
        at = pl.ds(pl.multiple_of(n1 * LANES, LANES), LANES)
        out[0, :, at] = jnp.where(low, a, roll_half(b)).astype(jnp.bfloat16)
        out[1, :, at] = jnp.where(low, roll_half(a), b).astype(jnp.bfloat16)
        return 0

    lax.fori_loop(0, first.shape[0], one, 0, unroll=16)


def assemble(first, second):
    block = ASSEMBLE
    return pl.pallas_call(
        assemble_kernel,
        grid=(RANGE_OUTER // block,),
        in_specs=[pl.BlockSpec((block, FRESH_ROWS, LANES), lambda i: (i, 0, 0))] * 2,
        out_specs=pl.BlockSpec((2, FRESH_ROWS, block * LANES), lambda i: (0, 0, i)),
        out_shape=jax.ShapeDtypeStruct((2, FRESH_ROWS, RANGE_BINS), jnp.bfloat16),
        compiler_params=pltpu.CompilerParams(
            dimension_semantics=("arbitrary",), vmem_limit_bytes=60 * MIB
        ),
        cost_estimate=pl.CostEstimate(
            flops=4 * FRESH_ROWS * RANGE_BINS, bytes_accessed=6 * MIB, transcendentals=0
        ),
        name="assemble",
    )(first, second)


def exchanged(blocks):
    return lax.all_to_all(blocks, AXES, split_axis=0, concat_axis=0, tiled=True)


def from_next(block):
    size = lax.axis_size(AXES)
    return lax.ppermute(block, AXES, [(i + 1, i) for i in range(size - 1)])


def on_device(
    slab_echoes,
    fresh_pulses,
    range_filter,
    azimuth_filter,
    migration_taps,
    band_offsets,
    band_widths,
):
    got = exchanged(range_compress(slab_echoes, fresh_pulses, range_filter))
    taps = migration_taps.reshape(BAND_MAX, PULSE_INNER, PULSE_OUTER)
    taps = taps.transpose(2, 1, 0).reshape(PULSES, BAND_MAX)
    filt, taps = prepare(azimuth_filter, taps)
    bands = jnp.stack([band_offsets, band_widths]).reshape(2, 2, 1, HALF)
    bands = jnp.broadcast_to(bands, (2, 2, 2, HALF)).reshape(2, 2, LANES)
    spectra0 = azimuth_forward(got, filt, 0)
    rim = from_next(spectra0)
    spectra1 = azimuth_forward(got, filt, 1)
    done0 = exchanged(azimuth_inverse(spectra0, spectra1, taps, bands[:, 0]))
    done1 = exchanged(azimuth_inverse(spectra1, rim, taps, bands[:, 1]))
    return assemble(done0, done1)


def solution(mesh):
    placed = (
        P(None, AXES, None),
        P(None, AXES, None),
        P(),
        P(None, None, AXES),
        P(),
        P(AXES),
        P(AXES),
    )
    return jax.shard_map(
        on_device,
        mesh=mesh,
        in_specs=placed,
        out_specs=P(None, AXES, None),
        check_vma=False,
    )
```

time: 259 us -> 182 us (0.70)
  Pallas kernels: 140 us -> 93.3 us
  blocking collectives: 75.8 us -> 29.9 us
  waiting for transfers between devices: 0.01 us -> 30.8 us
  local copies, waits for them, and re-layouts: 24.7 us -> 5.49 us
  starting transfers between devices: 17.4 us -> 21.5 us
    all_to_all x2 -> x1, blocking collectives: 75.8 us -> 29.9 us  [exchanged(): return lax.all_to_all(blocks, AXES, split_axis=0, concat_axis=0, tiled=True)]
    pallas_call x5, Pallas kernels: 107 us -> 75.6 us  [the longest x2 36.3 us: azimuth_inverse(): pl.pallas_call(inverse_kernel, in_specs=[in_hbm()] * 3 + [in_vmem(), in_h...]
    all_to_all x2, waiting for transfers between devices: 0.01 us -> 30.8 us  [exchanged(): return lax.all_to_all(blocks, AXES, split_axis=0, concat_axis=0, tiled=True)]
    unnamed x44 -> x9, local copies, waits for them, and re-layouts: 19.9 us -> 0.12 us
    pallas_call x1, Pallas kernels: 29.3 us -> 12.8 us  [range_compress(): pl.pallas_call(range_kernel, grid=(ROWS // STEP,), in_specs=[whole((2, ST...]
    all_to_all x2, starting transfers between devices: 14.4 us -> 18.3 us  [exchanged(): return lax.all_to_all(blocks, AXES, split_axis=0, concat_axis=0, tiled=True)]
  transfers between devices with their start and end apart: 3 -> 3, of which waited for: 0 -> 2; matrix products, arithmetic and copies ran while one was open for 2% -> 3% of each run, Pallas kernels for 41% -> 37%
where the time goes in v2:
time: 182 us; the launch traced here: 181 us
  Pallas kernels  93.3 us (51%)
  waiting for transfers between devices  30.8 us (17%)
  blocking collectives  29.9 us (16%)
  starting transfers between devices  21.5 us (12%)
  local copies, waits for them, and re-layouts  5.49 us (3%)
    pallas_call x2, Pallas kernels, azimuth_inverse(): pl.pallas_call(inverse_kernel, in_specs=[in_hbm()] * 3 + [in_vmem(), in_h...  36.3 us
    all_to_all x2, waiting for transfers between devices, exchanged(): return lax.all_to_all(blocks, AXES, split_axis=0, concat_axis=0, tiled=True)  30.8 us
    all_to_all x1, blocking collectives, exchanged(): return lax.all_to_all(blocks, AXES, split_axis=0, concat_axis=0, tiled=True)  29.9 us
    pallas_call x1, Pallas kernels, prepare(): pl.pallas_call(prepare_kernel, grid=(PULSE_OUTER // STEP,), in_specs=[pl....  23.1 us
    all_to_all x2, starting transfers between devices, exchanged(): return lax.all_to_all(blocks, AXES, split_axis=0, concat_axis=0, tiled=True)  18.3 us
    pallas_call x2, Pallas kernels, azimuth_forward(): pl.pallas_call(functools.partial(forward_kernel, half), in_specs=[in_hbm(...  16.1 us
    pallas_call x1, Pallas kernels, range_compress(): pl.pallas_call(range_kernel, grid=(ROWS // STEP,), in_specs=[whole((2, ST...  12.8 us
    pallas_call x1, Pallas kernels, assemble(): pl.pallas_call(assemble_kernel, grid=(RANGE_OUTER // block,), in_specs=[p...  4.86 us
  transfers between devices with their start and end apart: 3, of which 2 were waited for; matrix products, arithmetic and copies ran while one was open for 3% of the time, Pallas kernels for 37%

profile of v2, /device:TPU:1, one launch (start us, length us, event | category | flops | bytes accessed | tf_op | source)
XLA Modules:
  0.0 181.0 jit_solution(8611203427315225916)
XLA Ops:
  0.0 12.8 %range_compress.1 = bf16[128,2,64,128]{3,2,1,0:T(8,128)(2,1)} custom-call(bf16[2,16,16384]{2,1,0:T(8,128)(2,1)} %slab.1, bf16[2,48,16384]{2,1,0:T(8,128)(2,1)} %fresh.1, f32[2,16384]{1,0:T(2,128)} %filt.1, bf16[256,256]{1,0:T(8,128)(2,1)} %constant.18.clone.t1.t3, bf16[256,256]{1,0:T(8,128)(2,1)} %constant.19.clone.t2.t4, ...), custom_call_target="tpu_custom_call" | custom-call | flops 4294967296 | bytes 8388608 | tf_op jit(solution)/shard_map/range_compress/pallas_call | solution.py:222
  12.8 0.0 copy-start.1
  12.8 12.0 %all-to-all-start = ((bf16[128,2,64,128]{3,2,1,0:T(8,128)(2,1)}), bf16[128,2,64,128]{3,2,1,0:T(8,128)(2,1)}, u32[]{:S(2)}, u32[]{:S(2)}) async-start(bf16[128,2,64,128]{3,2,1,0:T(8,128)(2,1)} %range_compress.1), calls=%async_computation | async-start | bytes 8388608 | tf_op jit(solution)/shard_map/all_to_all | solution.py:587
  24.8 0.0 copy-done.1
  24.8 0.1 copy.26
  24.9 4.5 %copy.24 = f32[9,64,128]{0,1,2:T(8,128)} copy(f32[9,64,128]{2,1,0:T(8,128)S(1)} %slice.10) | data formatting | bytes 589824 | tf_op jit(solution)/shard_map/reshape | solution.py:605
  29.4 23.1 %prepare.1 = (bf16[2,2,8192,128]{3,2,1,0:T(8,128)(2,1)}, bf16[9,8192,128]{2,1,0:T(8,128)(2,1)}) custom-call(bf16[2,64,128,128]{3,2,1,0:T(8,128)(2,1)} %bitcast.16, f32[8192,9]{1,0:T(8,128)} %bitcast.15), custom_call_target="tpu_custom_call" | custom-call | flops 8388608 | bytes 35651584 | tf_op jit(solution)/shard_map/prepare/pallas_call | solution.py:282
  52.6 24.2 %all-to-all-done.got_hbm = bf16[128,2,64,128]{3,2,1,0:T(8,128)(2,1)} async-done(((bf16[128,2,64,128]{3,2,1,0:T(8,128)(2,1)}), bf16[128,2,64,128]{3,2,1,0:T(8,128)(2,1)}, u32[]{:S(2)}, u32[]{:S(2)}) %all-to-all-start) | async-done | bytes 4194336 | tf_op jit(solution)/shard_map/all_to_all | solution.py:587
  76.7 0.0 copy-start.2
  76.7 0.0 copy-start.3
  76.7 8.1 %azimuth_forward.2.left_hbm = bf16[8192,128]{1,0:T(8,128)(2,1)} custom-call(bf16[128,2,64,128]{3,2,1,0:T(8,128)(2,1)} %all-to-all-done.got_hbm, bf16[64,128,256]{2,1,0:T(8,128)(2,1)} %constant.22.clone.g1_hbm, bf16[128,128]{1,0:T(8,128)(2,1)} %constant.23.clone.t2, bf16[2,2,8192,128]{3,2,1,0:T(8,128)(2,1)} %get-tuple-element.7.filt_hbm), custom_call_target="tpu_custom_call" | custom-call | flops 1073741824 | bytes 12582912 | tf_op jit(solution)/shard_map/azimuth_forward/pallas_call | solution.py:386
  84.8 3.1 %collective-permute-start = (bf16[8192,128]{1,0:T(8,128)(2,1)}, bf16[8192,128]{1,0:T(8,128)(2,1)}, u32[]{:S(2)}, u32[]{:S(2)}) collective-permute-start(bf16[8192,128]{1,0:T(8,128)(2,1)} %azimuth_forward.2.left_hbm), channel_id=1, source_target_pairs={{1,0},{2,1},{3,2},{4,3},{5,4},{6,5},{7,6},{8,7},{9,8},{10,9},{11,1... | collective-permute-start | bytes 6291464 | tf_op jit(solution)/shard_map/ppermute | solution.py:592
  87.9 0.0 copy-done.2
  88.0 0.1 stack.10
  88.0 0.0 copy-done.3
  88.0 0.1 stack.9
  88.1 0.1 reshape.20
  88.2 0.6 slice_bitcast_fusion
  88.8 8.1 %azimuth_forward.3.right_hbm.left_hbm = bf16[8192,128]{1,0:T(8,128)(2,1)} custom-call(bf16[128,2,64,128]{3,2,1,0:T(8,128)(2,1)} %all-to-all-done.got_hbm, bf16[64,128,256]{2,1,0:T(8,128)(2,1)} %constant.22.clone.g1_hbm, bf16[128,128]{1,0:T(8,128)(2,1)} %constant.23.clone.t2, bf16[2,2,8192,128]{3,2,1,0:T(8,128)(2,1)} %get-tuple-element.7.filt_hbm), custom_call_target="tpu_custom_call" | custom-call | flops 1073741824 | bytes 12582912 | tf_op jit(solution)/shard_map/azimuth_forward/pallas_call | solution.py:386
  96.9 18.2 %migrate_inverse.2 = bf16[128,48,128]{2,1,0:T(8,128)(2,1)} custom-call(bf16[8192,128]{1,0:T(8,128)(2,1)} %azimuth_forward.2.left_hbm, bf16[8192,128]{1,0:T(8,128)(2,1)} %azimuth_forward.3.right_hbm.left_hbm, bf16[9,8192,128]{2,1,0:T(8,128)(2,1)} %get-tuple-element.8.taps_hbm, s32[2,128]{1,0:T(2,128)} %get-tuple-element.10.bands, ...), custom_call_target="tpu_custom_call" | custom-call | flops 5905580032 | bytes 12582912 | tf_op jit(solution)/shard_map/migrate_inverse/pallas_call | solution.py:526
  115.1 6.4 %all-to-all-start.1 = ((bf16[128,48,128]{2,1,0:T(8,128)(2,1)}), bf16[128,48,128]{2,1,0:T(8,128)(2,1)S(1)}, u32[]{:S(2)}, u32[]{:S(2)}) async-start(bf16[128,48,128]{2,1,0:T(8,128)(2,1)} %migrate_inverse.2), calls=%async_computation.1 | async-start | bytes 3145728 | tf_op jit(solution)/shard_map/all_to_all | solution.py:587
  121.5 0.0 collective-permute-done.right_hbm
  121.5 18.1 %migrate_inverse.3 = bf16[128,48,128]{2,1,0:T(8,128)(2,1)} custom-call(bf16[8192,128]{1,0:T(8,128)(2,1)} %azimuth_forward.3.right_hbm.left_hbm, bf16[8192,128]{1,0:T(8,128)(2,1)} %collective-permute-done.right_hbm, bf16[9,8192,128]{2,1,0:T(8,128)(2,1)} %get-tuple-element.8.taps_hbm, s32[2,128]{1,0:T(2,128)} %get-tuple-element.9.bands, ...), custom_call_target="tpu_custom_call" | custom-call | flops 5905580032 | bytes 12582912 | tf_op jit(solution)/shard_map/migrate_inverse/pallas_call | solution.py:526
  139.6 6.6 %all-to-all-done.1.first = bf16[128,48,128]{2,1,0:T(8,128)(2,1)S(1)} async-done(((bf16[128,48,128]{2,1,0:T(8,128)(2,1)}), bf16[128,48,128]{2,1,0:T(8,128)(2,1)S(1)}, u32[]{:S(2)}, u32[]{:S(2)}) %all-to-all-start.1) | async-done | bytes 1572896 | tf_op jit(solution)/shard_map/all_to_all | solution.py:587
  146.2 0.0 copy-start
  146.2 29.9 %all_to_all.15.second = bf16[128,48,128]{2,1,0:T(8,128)(2,1)} all-to-all(bf16[128,48,128]{2,1,0:T(8,128)(2,1)} %migrate_inverse.3), channel_id=1, replica_groups=mesh['az'=8,'rg'=16] {'az','rg'}, dimensions={0} | all-to-all | bytes 3145728 | tf_op jit(solution)/shard_map/all_to_all | solution.py:587
  176.1 0.0 copy-done
  176.1 4.9 %assemble.1 = bf16[2,48,16384]{2,1,0:T(8,128)(2,1)} custom-call(bf16[128,48,128]{2,1,0:T(8,128)(2,1)} %copy-done, bf16[128,48,128]{2,1,0:T(8,128)(2,1)} %all_to_all.15.second), custom_call_target="tpu_custom_call" | custom-call | flops 3145728 | bytes 6291456 | tf_op jit(solution)/shard_map/assemble/pallas_call | solution.py:570
  (4 shorter events, 0.0 us)
Async XLA Ops:
  12.8 12.0 %copy-start.1 = (f32[9,8192]{1,0:T(8,128)S(1)}, f32[9,8192]{1,0:T(8,128)}, u32[]{:S(2)}) copy-start(f32[9,8192]{1,0:T(8,128)} %param.27) | copy-start | bytes 884740
  12.8 63.9 %all-to-all-start = ((bf16[128,2,64,128]{3,2,1,0:T(8,128)(2,1)}), bf16[128,2,64,128]{3,2,1,0:T(8,128)(2,1)}, u32[]{:S(2)}, u32[]{:S(2)}) async-start(bf16[128,2,64,128]{3,2,1,0:T(8,128)(2,1)} %range_compress.1), calls=%async_computation | async-start | bytes 8388608 | tf_op jit(solution)/shard_map/all_to_all | solution.py:587
  76.7 11.2 %copy-start.2 = (s32[128]{0:T(128)S(1)}, s32[128]{0:T(128)}, u32[]{:S(2)}) copy-start(s32[128]{0:T(128)} %param.29) | copy-start | bytes 1540
  76.7 11.3 %copy-start.3 = (s32[128]{0:T(128)S(1)}, s32[128]{0:T(128)}, u32[]{:S(2)}) copy-start(s32[128]{0:T(128)} %param.28) | copy-start | bytes 1540
  84.8 36.7 %collective-permute-start = (bf16[8192,128]{1,0:T(8,128)(2,1)}, bf16[8192,128]{1,0:T(8,128)(2,1)}, u32[]{:S(2)}, u32[]{:S(2)}) collective-permute-start(bf16[8192,128]{1,0:T(8,128)(2,1)} %azimuth_forward.2.left_hbm), channel_id=1, source_target_pairs={{1,0},{2,1},{3,2},{4,3},{5,4},{6,5},{7,6},{8,7},{9,8},{10,9},{11,1... | collective-permute-start | bytes 6291464 | tf_op jit(solution)/shard_map/ppermute | solution.py:592
  115.1 31.2 %all-to-all-start.1 = ((bf16[128,48,128]{2,1,0:T(8,128)(2,1)}), bf16[128,48,128]{2,1,0:T(8,128)(2,1)S(1)}, u32[]{:S(2)}, u32[]{:S(2)}) async-start(bf16[128,48,128]{2,1,0:T(8,128)(2,1)} %migrate_inverse.2), calls=%async_computation.1 | async-start | bytes 3145728 | tf_op jit(solution)/shard_map/all_to_all | solution.py:587
  146.2 29.9 %copy-start = (bf16[128,48,128]{2,1,0:T(8,128)(2,1)}, bf16[128,48,128]{2,1,0:T(8,128)(2,1)S(1)}, u32[]{:S(2)}) copy-start(bf16[128,48,128]{2,1,0:T(8,128)(2,1)S(1)} %all-to-all-done.1.first) | copy-start | bytes 4718596

commit v3 on v2

--- a/solution.py
+++ b/solution.py
@@ -30,7 +30,7 @@
 KEPT_OUTER = PULSE_OUTER - FIRST_OUTER
 GROUP = 4
 UNROLL = 8
-PITCH = STEP + 8
+PITCH = STEP + 4
 INNER_PITCH = PULSE_INNER + 8
 OUTER_PITCH = PULSE_OUTER + 8
 BLOCKS = ROWS // STEP
@@ -38,7 +38,7 @@
 FWD_LIMIT = 60
 INV_LIMIT = 60
 PARTS = 4
-ASSEMBLE = 32
+SPREAD = 6
 AXES = ("az", "rg")
 MIB = 1024 * 1024
 
@@ -86,11 +86,6 @@
     )
 
 
-def turn_table():
-    one = np.eye(HALF, dtype=np.float32)
-    return bf16(np.block([[0 * one, one], [-one, 0 * one]]))
-
-
 def roll_half(values):
     return pltpu.roll(values, HALF, 1)
 
@@ -104,6 +99,10 @@
     return jnp.where(lane_ids(values.shape[0]) < HALF, -turned, turned)
 
 
+def with_i(values):
+    return jnp.concatenate([values, times_i(values)], axis=0)
+
+
 def dot(left, right):
     return jnp.dot(left, right, preferred_element_type=jnp.float32)
 
@@ -122,7 +121,7 @@
     def load(source):
         def one(n1, _):
             at = pl.ds(pl.multiple_of(n1 * LANES, LANES), LANES)
-            to = pl.ds(pl.multiple_of(n1 * PITCH, 8), STEP)
+            to = pl.ds(pl.multiple_of(n1 * PITCH, 4), STEP)
             for c in range(2):
                 xs[c, to, :] = source[c, :, at].astype(jnp.float32)
             return 0
@@ -195,7 +194,7 @@
         lax.fori_loop(0, STEP // 2, stage, 0, unroll=UNROLL)
 
     def store(n1, _):
-        at = pl.ds(pl.multiple_of(n1 * PITCH, 8), STEP)
+        at = pl.ds(pl.multiple_of(n1 * PITCH, 4), STEP)
         out[n1, 0] = os[0, at, :].astype(jnp.bfloat16)
         out[n1, 1] = os[1, at, :].astype(jnp.bfloat16)
         return 0
@@ -253,7 +252,8 @@
     )(slab, fresh, range_filter, *tables, w_in, w_out)
 
 
-def prepare_kernel(filt, taps, out, wide, fs):
+def prepare_kernel(filt, taps, out, narrow, wide, fs):
+    narrow[:, :BAND_MAX] = taps[...].astype(jnp.bfloat16)
     for c in range(2):
         for kl in range(PULSE_INNER):
             fs[c, kl * PITCH : kl * PITCH + STEP, :] = filt[c, kl].astype(jnp.float32)
@@ -268,7 +268,7 @@
 
     def spread(i, _):
         at = pl.ds(pl.multiple_of(i * STEP, STEP), STEP)
-        for j in range(BAND_MAX):
+        for j in range(SPREAD):
             column = jnp.broadcast_to(taps[at, j : j + 1], (STEP, LANES))
             wide[j, at, :] = column.astype(jnp.bfloat16)
         return 0
@@ -288,11 +288,13 @@
         ],
         out_specs=[
             pl.BlockSpec((2, 2, rows, LANES), lambda i: (0, 0, i, 0)),
-            pl.BlockSpec((BAND_MAX, rows, LANES), lambda i: (0, i, 0)),
+            pl.BlockSpec((rows, LANES), lambda i: (i, 0)),
+            pl.BlockSpec((SPREAD, rows, LANES), lambda i: (0, i, 0)),
         ],
         out_shape=[
             jax.ShapeDtypeStruct((2, 2, PULSES, LANES), jnp.bfloat16),
-            jax.ShapeDtypeStruct((BAND_MAX, PULSES, LANES), jnp.bfloat16),
+            jax.ShapeDtypeStruct((PULSES, LANES), jnp.bfloat16),
+            jax.ShapeDtypeStruct((SPREAD, PULSES, LANES), jnp.bfloat16),
         ],
         scratch_shapes=[pltpu.VMEM((2, PULSE_INNER * PITCH, LANES), jnp.float32)],
         compiler_params=pltpu.CompilerParams(
@@ -312,13 +314,17 @@
     return copies
 
 
-def forward_kernel(
-    half, got_hbm, g1_hbm, t2, filt_hbm, out_hbm, got, g1, filt, out, ps, ts, sems, out_sems
-):
-    get_got, get_g1, get_filt = start_all(
-        ((got_hbm.at[:, half], got), (g1_hbm, g1), (filt_hbm.at[half], filt)), sems
-    )
-    get_got.wait()
+def then_start(copy, others):
+    def run():
+        copy.wait()
+        for other in others:
+            other.start()
+
+    return run
+
+
+def forward_steps(got, g1, t2, filt, out, ps, ts, waits):
+    waits[0]()
     quarter = PULSE_INNER // STEP
     fresh_units = FRESH_ROWS // STEP
 
@@ -338,11 +344,11 @@
 
     def outer(l, _):
         x = ps[pl.ds(l, PULSE_OUTER, stride=INNER_PITCH), :]
-        both = jnp.concatenate([x.astype(jnp.bfloat16), times_i(x).astype(jnp.bfloat16)], axis=0)
+        both = with_i(x.astype(jnp.bfloat16))
         ts[pl.ds(l, PULSE_OUTER, stride=INNER_PITCH), :] = dot(g1[l], both)
         return 0
 
-    get_g1.wait()
+    waits[1]()
     lax.fori_loop(0, PULSE_INNER, outer, 0, unroll=16)
 
     def inner(i, _):
@@ -351,7 +357,7 @@
             at = pl.ds(pl.multiple_of((2 * i + k) * INNER_PITCH, 8), PULSE_INNER)
             t = ts[at, :]
             sides.append(
-                jnp.concatenate([t.astype(jnp.bfloat16), times_i(t).astype(jnp.bfloat16)], axis=0)
+                with_i(t.astype(jnp.bfloat16))
             )
         y = dot(t2[...], jnp.concatenate(sides, axis=1))
         for k in range(2):
@@ -363,7 +369,17 @@
             ).astype(jnp.bfloat16)
         return 0
 
-    get_filt.wait()
+    waits[2]()
+    return inner
+
+
+def forward_kernel(
+    half, got_hbm, g1_hbm, t2, filt_hbm, out_hbm, got, g1, filt, out, ps, ts, sems, out_sems
+):
+    copies = start_all(((got_hbm.at[:, half], got), (g1_hbm, g1)), sems)
+    last = pltpu.make_async_copy(filt_hbm.at[half], filt, sems.at[2])
+    waits = [then_start(copies[0], [last]), copies[1].wait, last.wait]
+    inner = forward_steps(got, g1, t2, filt, out, ps, ts, waits)
     put_in_parts(inner, PULSE_OUTER // 2, 16, out, out_hbm, out_sems)
 
 
@@ -380,9 +396,7 @@
 
 
 def azimuth_forward(got, filt, half):
-    g1 = turned_tables(PULSE_OUTER, PULSE_INNER, -1.0)
-    re, im = dft_table(PULSE_INNER, -1.0)
-    t2 = bf16(np.block([[re, im], [-im, re]]))
+    g1, t2 = forward_tables()
     return pl.pallas_call(
         functools.partial(forward_kernel, half),
         in_specs=[in_hbm(), in_hbm(), in_vmem(), in_hbm()],
@@ -406,17 +420,116 @@
     )(got, g1, t2, filt)
 
 
+def tap_steps():
+    later = [(j, min(2, BAND_MAX - j)) for j in range(SPREAD, BAND_MAX, 2)]
+    return later + [(j, 2) for j in range(0, SPREAD, 2)]
+
+
+def tap_pairs(narrow_hbm, narrow, taps_hbm, taps):
+    spans = [pl.ds(j, 2) for j in range(0, SPREAD, 2)]
+    return [(narrow_hbm, narrow)] + [(taps_hbm.at[at], taps.at[at]) for at in spans]
+
+
+def select_table(half, bands, sel):
+    index = lax.broadcasted_iota(jnp.int32, (2 * LANES, LANES), 0)
+    lane = lax.broadcasted_iota(jnp.int32, (2 * LANES, LANES), 1)
+    column = jnp.where(index >= LANES, HALF, 0) + (index & (HALF - 1))
+    same = ((index >> 6) & 1) == (lane >> 6)
+    want = (lane & (HALF - 1)) + bands[half : half + 1, :]
+    for j in range(BAND_MAX):
+        hit = same & (column == want + j) & (bands[2 + half : 3 + half, :] > j)
+        sel[:, j * LANES : (j + 1) * LANES] = jnp.where(hit, 1.0, 0.0).astype(jnp.bfloat16)
+
+
+def inverse_steps(
+    left, right, narrow, taps, sel, g1, t2, out, out_hbm, sums, moved, vs, os, waits, out_sems
+):
+    size = GROUP * PULSE_INNER
+
+    steps = tap_steps()
+
+    def pick(order, g, _):
+        j, wide = steps[order]
+        at = pl.ds(pl.multiple_of(g * size, size), size)
+        source = jnp.concatenate([left[at, :], right[at, :]], axis=1)
+        picked = dot(source, sel[:, j * LANES : (j + wide) * LANES])
+        total = None if order == 0 else sums[at, :]
+        if j >= SPREAD:
+            columns = narrow[at, :].astype(jnp.float32)
+        for k in range(wide):
+            if j >= SPREAD:
+                weight = columns[:, j + k : j + k + 1]
+            else:
+                weight = taps[j + k, at, :].astype(jnp.float32)
+            term = picked[:, k * LANES : (k + 1) * LANES] * weight
+            total = term if total is None else total + term
+        if order + 1 < len(steps):
+            sums[at, :] = total
+        else:
+            moved[at, :] = total.astype(jnp.bfloat16)
+        return 0
+
+    waits[0]()
+    waits[1]()
+    for order, (j, _) in enumerate(steps):
+        if j < SPREAD:
+            waits[2 + j // 2]()
+        lax.fori_loop(0, PULSE_OUTER // GROUP, functools.partial(pick, order), 0, unroll=32)
+
+    def inner(kb, _):
+        at = pl.ds(pl.multiple_of(kb * PULSE_INNER, PULSE_INNER), PULSE_INNER)
+        vs[pl.ds(kb, PULSE_INNER, stride=OUTER_PITCH), :] = dot(g1[kb], with_i(moved[at, :]))
+        return 0
+
+    waits[-1]()
+    lax.fori_loop(0, PULSE_OUTER, inner, 0, unroll=32)
+
+    def last(i, _):
+        sides = []
+        for k in range(2):
+            at = pl.ds(pl.multiple_of((2 * i + k) * OUTER_PITCH, 8), PULSE_OUTER)
+            v = vs[at, :]
+            sides.append(
+                with_i(v.astype(jnp.bfloat16))
+            )
+        y = dot(t2[...], jnp.concatenate(sides, axis=1))
+        for k in range(2):
+            os[pl.ds(2 * i + k, KEPT_OUTER, stride=INNER_PITCH), :] = y[
+                :, k * LANES : (k + 1) * LANES
+            ]
+        return 0
+
+    lax.fori_loop(0, PULSE_INNER // 2, last, 0, unroll=8)
+
+    quarter = PULSE_INNER // STEP
+    fresh_units = FRESH_ROWS // STEP
+
+    def pack(g, _):
+        base = pl.multiple_of(g * fresh_units * INNER_PITCH, 8)
+        for d in range(quarter):
+            for k in range(fresh_units):
+                unit = d * fresh_units + k
+                at = (unit // quarter) * INNER_PITCH + (unit % quarter) * STEP
+                out[g * quarter + d, k * STEP : (k + 1) * STEP, :] = os[
+                    pl.ds(base + at, STEP), :
+                ].astype(jnp.bfloat16)
+        return 0
+
+    put_in_parts(pack, DEVICES // quarter, 4, out, out_hbm, out_sems)
+
+
 def inverse_kernel(
     left_hbm,
     right_hbm,
+    narrow_hbm,
     taps_hbm,
     bands,
     g1_hbm,
     t2,
-    by_i,
     out_hbm,
     left,
     right,
+    narrow,
     taps,
     g1,
     out,
@@ -428,118 +541,150 @@
     sems,
     out_sems,
 ):
-    starts = range(0, BAND_MAX, 2)
-    pairs = [(left_hbm, left), (right_hbm, right)]
-    for j in starts:
-        at = pl.ds(j, min(2, BAND_MAX - j))
-        pairs.append((taps_hbm.at[at], taps.at[at]))
-    copies = start_all([*pairs, (g1_hbm, g1)], sems)
-
-    index = lax.broadcasted_iota(jnp.int32, (2 * LANES, LANES), 0)
-    lane = lax.broadcasted_iota(jnp.int32, (2 * LANES, LANES), 1)
-    column = jnp.where(index >= LANES, HALF, 0) + (index & (HALF - 1))
-    same = ((index >> 6) & 1) == (lane >> 6)
-    want = (lane & (HALF - 1)) + bands[0:1, :]
-    for j in range(BAND_MAX):
-        hit = same & (column == want + j) & (bands[1:2, :] > j)
-        sel[:, j * LANES : (j + 1) * LANES] = jnp.where(hit, 1.0, 0.0).astype(jnp.bfloat16)
-
-    size = GROUP * PULSE_INNER
-
-    def pick(j, g, _):
-        at = pl.ds(pl.multiple_of(g * size, size), size)
-        wide = min(2, BAND_MAX - j)
-        source = jnp.concatenate([left[at, :], right[at, :]], axis=1)
-        picked = dot(source, sel[:, j * LANES : (j + wide) * LANES])
-        total = None if j == 0 else sums[at, :]
-        for k in range(wide):
-            weight = taps[j + k, at, :].astype(jnp.float32)
-            term = picked[:, k * LANES : (k + 1) * LANES] * weight
-            total = term if total is None else total + term
-        if j + wide < BAND_MAX:
-            sums[at, :] = total
-            return 0
-        here = total.astype(jnp.bfloat16)
-        for k in range(GROUP):
-            moved[g * GROUP + k, :PULSE_INNER, :] = here[k * PULSE_INNER : (k + 1) * PULSE_INNER]
-        return 0
-
-    def turn(g, _):
-        here = [moved[g * GROUP + k, :PULSE_INNER, :] for k in range(GROUP)]
-        turned = dot(jnp.concatenate(here, axis=0), by_i[...]).astype(jnp.bfloat16)
-        for k in range(GROUP):
-            moved[g * GROUP + k, PULSE_INNER:, :] = turned[k * PULSE_INNER : (k + 1) * PULSE_INNER]
-        return 0
-
-    copies[0].wait()
-    copies[1].wait()
-    for j in starts:
-        copies[2 + j // 2].wait()
-        lax.fori_loop(0, PULSE_OUTER // GROUP, functools.partial(pick, j), 0, unroll=16)
-    lax.fori_loop(0, PULSE_OUTER // GROUP, turn, 0, unroll=8)
-
-    def inner(kb, _):
-        vs[pl.ds(kb, PULSE_INNER, stride=OUTER_PITCH), :] = dot(g1[kb], moved[kb])
-        return 0
-
-    copies[-1].wait()
-    lax.fori_loop(0, PULSE_OUTER, inner, 0, unroll=16)
-
-    def last(i, _):
-        sides = []
-        for k in range(2):
-            at = pl.ds(pl.multiple_of((2 * i + k) * OUTER_PITCH, 8), PULSE_OUTER)
-            v = vs[at, :]
-            sides.append(
-                jnp.concatenate([v.astype(jnp.bfloat16), times_i(v).astype(jnp.bfloat16)], axis=0)
-            )
-        y = dot(t2[...], jnp.concatenate(sides, axis=1))
-        for k in range(2):
-            os[pl.ds(2 * i + k, KEPT_OUTER, stride=INNER_PITCH), :] = y[
-                :, k * LANES : (k + 1) * LANES
-            ]
-        return 0
-
-    lax.fori_loop(0, PULSE_INNER // 2, last, 0, unroll=8)
-
-    quarter = PULSE_INNER // STEP
-    fresh_units = FRESH_ROWS // STEP
-
-    def pack(g, _):
-        base = pl.multiple_of(g * fresh_units * INNER_PITCH, 8)
-        for d in range(quarter):
-            for k in range(fresh_units):
-                unit = d * fresh_units + k
-                at = (unit // quarter) * INNER_PITCH + (unit % quarter) * STEP
-                out[g * quarter + d, k * STEP : (k + 1) * STEP, :] = os[
-                    pl.ds(base + at, STEP), :
-                ].astype(jnp.bfloat16)
-        return 0
-
-    put_in_parts(pack, DEVICES // quarter, 4, out, out_hbm, out_sems)
-
-
-def azimuth_inverse(left, right, taps, bands):
-    g1 = turned_tables(PULSE_INNER, PULSE_OUTER, 1.0)
+    pairs = [(left_hbm, left), (right_hbm, right), *tap_pairs(narrow_hbm, narrow, taps_hbm, taps), (g1_hbm, g1)]
+    copies = start_all(pairs, sems)
+    select_table(1, bands, sel)
+
+    def both():
+        copies[0].wait()
+        copies[1].wait()
+
+    waits = [both, *[copy.wait for copy in copies[2:]]]
+    inverse_steps(
+        left, right, narrow, taps, sel, g1, t2, out, out_hbm, sums, moved, vs, os, waits, out_sems
+    )
+
+
+def middle_kernel(
+    half,
+    got_hbm,
+    f1_hbm,
+    f2,
+    filt_hbm,
+    left_hbm,
+    narrow_hbm,
+    taps_hbm,
+    bands,
+    g1_hbm,
+    t2,
+    right_hbm,
+    out_hbm,
+    got,
+    f1,
+    filt,
+    right,
+    ps,
+    ts,
+    left,
+    narrow,
+    taps,
+    g1,
+    out,
+    sel,
+    sums,
+    moved,
+    sems,
+    late_sems,
+    right_sem,
+    out_sems,
+):
+    first = start_all(((got_hbm.at[:, half], got), (f1_hbm, f1)), sems)
+    first.append(pltpu.make_async_copy(filt_hbm.at[half], filt, sems.at[2]))
+    pairs = [(left_hbm, left), *tap_pairs(narrow_hbm, narrow, taps_hbm, taps), (g1_hbm, g1)]
+    late = [pltpu.make_async_copy(a, b, late_sems.at[i]) for i, (a, b) in enumerate(pairs)]
+    select_table(0, bands, sel)
+
+    cut = 4
+    waits = [
+        then_start(first[0], first[2:]),
+        then_start(first[1], late[:cut]),
+        then_start(first[2], late[cut:]),
+    ]
+    inner = forward_steps(got, f1, f2, filt, right, ps, ts, waits)
+    lax.fori_loop(0, PULSE_OUTER // 2, inner, 0, unroll=16)
+    put_right = pltpu.make_async_copy(right, right_hbm, right_sem.at[0])
+    put_right.start()
+    waits = [copy.wait for copy in late]
+    inverse_steps(
+        left, right, narrow, taps, sel, g1, t2, out, out_hbm, sums, moved, ts, ps, waits, out_sems
+    )
+    put_right.wait()
+
+
+def forward_tables():
+    re, im = dft_table(PULSE_INNER, -1.0)
+    t2 = bf16(np.block([[re, im], [-im, re]]))
+    return turned_tables(PULSE_OUTER, PULSE_INNER, -1.0), t2
+
+
+def inverse_tables():
     re, im = dft_table(PULSE_OUTER, 1.0)
     t2 = bf16(np.concatenate([re[FIRST_OUTER:], im[FIRST_OUTER:]], axis=1))
+    return turned_tables(PULSE_INNER, PULSE_OUTER, 1.0), t2
+
+
+def forward_and_inverse(got, filt, half, left, narrow, taps, bands):
+    f1, f2 = forward_tables()
+    g1, t2 = inverse_tables()
     return pl.pallas_call(
-        inverse_kernel,
-        in_specs=[in_hbm()] * 3 + [in_vmem(), in_hbm(), in_vmem(), in_vmem()],
-        out_specs=in_hbm(),
-        out_shape=jax.ShapeDtypeStruct((DEVICES, FRESH_ROWS, LANES), jnp.bfloat16),
+        functools.partial(middle_kernel, half),
+        in_specs=[in_hbm(), in_hbm(), in_vmem()] + [in_hbm()] * 4
+        + [in_vmem(), in_hbm(), in_vmem()],
+        out_specs=[in_hbm(), in_hbm()],
+        out_shape=[
+            jax.ShapeDtypeStruct((PULSES, LANES), jnp.bfloat16),
+            jax.ShapeDtypeStruct((DEVICES, FRESH_ROWS, LANES), jnp.bfloat16),
+        ],
         scratch_shapes=[
-            pltpu.VMEM((PULSES, LANES), jnp.bfloat16),
-            pltpu.VMEM((PULSES, LANES), jnp.bfloat16),
-            pltpu.VMEM((BAND_MAX, PULSES, LANES), jnp.bfloat16),
+            pltpu.VMEM((DEVICES, ROWS, LANES), jnp.bfloat16),
+            pltpu.VMEM(f1.shape, jnp.bfloat16),
+            pltpu.VMEM((2, PULSES, LANES), jnp.bfloat16),
+            pltpu.VMEM((PULSES, LANES), jnp.bfloat16),
+            pltpu.VMEM((PULSE_OUTER * INNER_PITCH, LANES), jnp.float32),
+            pltpu.VMEM((PULSE_OUTER * INNER_PITCH, LANES), jnp.float32),
+            pltpu.VMEM((PULSES, LANES), jnp.bfloat16),
+            pltpu.VMEM((PULSES, LANES), jnp.bfloat16),
+            pltpu.VMEM((SPREAD, PULSES, LANES), jnp.bfloat16),
             pltpu.VMEM(g1.shape, jnp.bfloat16),
             pltpu.VMEM((DEVICES, FRESH_ROWS, LANES), jnp.bfloat16),
             pltpu.VMEM((2 * LANES, BAND_MAX * LANES), jnp.bfloat16),
             pltpu.VMEM((PULSES, LANES), jnp.float32),
-            pltpu.VMEM((PULSE_OUTER, 2 * PULSE_INNER, LANES), jnp.bfloat16),
+            pltpu.VMEM((PULSES, LANES), jnp.bfloat16),
+            pltpu.SemaphoreType.DMA((3,)),
+            pltpu.SemaphoreType.DMA((3 + SPREAD // 2,)),
+            pltpu.SemaphoreType.DMA((1,)),
+            pltpu.SemaphoreType.DMA((PARTS,)),
+        ],
+        compiler_params=pltpu.CompilerParams(vmem_limit_bytes=INV_LIMIT * MIB),
+        cost_estimate=pl.CostEstimate(
+            flops=2 * PULSES * LANES * (256 * BAND_MAX + 1024),
+            bytes_accessed=40 * MIB,
+            transcendentals=0,
+        ),
+        name="forward_inverse",
+    )(got, f1, f2, filt, left, narrow, taps, bands, g1, t2)
+
+
+def azimuth_inverse(left, right, narrow, taps, bands):
+    g1, t2 = inverse_tables()
+    return pl.pallas_call(
+        inverse_kernel,
+        in_specs=[in_hbm()] * 4 + [in_vmem(), in_hbm(), in_vmem()],
+        out_specs=in_hbm(),
+        out_shape=jax.ShapeDtypeStruct((DEVICES, FRESH_ROWS, LANES), jnp.bfloat16),
+        scratch_shapes=[
+            pltpu.VMEM((PULSES, LANES), jnp.bfloat16),
+            pltpu.VMEM((PULSES, LANES), jnp.bfloat16),
+            pltpu.VMEM((PULSES, LANES), jnp.bfloat16),
+            pltpu.VMEM((SPREAD, PULSES, LANES), jnp.bfloat16),
+            pltpu.VMEM(g1.shape, jnp.bfloat16),
+            pltpu.VMEM((DEVICES, FRESH_ROWS, LANES), jnp.bfloat16),
+            pltpu.VMEM((2 * LANES, BAND_MAX * LANES), jnp.bfloat16),
+            pltpu.VMEM((PULSES, LANES), jnp.float32),
+            pltpu.VMEM((PULSES, LANES), jnp.bfloat16),
             pltpu.VMEM((PULSE_INNER * OUTER_PITCH, LANES), jnp.float32),
             pltpu.VMEM((KEPT_OUTER * INNER_PITCH, LANES), jnp.float32),
-            pltpu.SemaphoreType.DMA((3 + (BAND_MAX + 1) // 2,)),
+            pltpu.SemaphoreType.DMA((4 + SPREAD // 2,)),
             pltpu.SemaphoreType.DMA((PARTS,)),
         ],
         compiler_params=pltpu.CompilerParams(vmem_limit_bytes=INV_LIMIT * MIB),
@@ -549,11 +694,15 @@
             transcendentals=0,
         ),
         name="migrate_inverse",
-    )(left, right, taps, bands, g1, t2, turn_table())
-
-
-def assemble_kernel(first, second, out):
+    )(left, right, narrow, taps, bands, g1, t2)
+
+
+def assemble_kernel(first_hbm, second_hbm, out_hbm, first, second, out, sems, more_sems, out_sems):
     low = lane_ids(FRESH_ROWS) < HALF
+    size = RANGE_OUTER // PARTS
+    spans = [pl.ds(i * size, size) for i in range(PARTS)]
+    copies = start_all([(first_hbm.at[at], first.at[at]) for at in spans], sems)
+    more = start_all([(second_hbm.at[at], second.at[at]) for at in spans], more_sems)
 
     def one(n1, _):
         a, b = first[n1].astype(jnp.float32), second[n1].astype(jnp.float32)
@@ -562,20 +711,35 @@
         out[1, :, at] = jnp.where(low, roll_half(a), b).astype(jnp.bfloat16)
         return 0
 
-    lax.fori_loop(0, first.shape[0], one, 0, unroll=16)
+    puts = []
+    for i in range(PARTS):
+        copies[i].wait()
+        more[i].wait()
+        lax.fori_loop(i * size, (i + 1) * size, one, 0, unroll=16)
+        at = pl.ds(i * size * LANES, size * LANES)
+        puts.append(pltpu.make_async_copy(out.at[:, :, at], out_hbm.at[:, :, at], out_sems.at[i]))
+        puts[i].start()
+    for put in puts:
+        put.wait()
 
 
 def assemble(first, second):
-    block = ASSEMBLE
+    part = pltpu.VMEM((RANGE_OUTER, FRESH_ROWS, LANES), jnp.bfloat16)
+    shape = (2, FRESH_ROWS, RANGE_BINS)
     return pl.pallas_call(
         assemble_kernel,
-        grid=(RANGE_OUTER // block,),
-        in_specs=[pl.BlockSpec((block, FRESH_ROWS, LANES), lambda i: (i, 0, 0))] * 2,
-        out_specs=pl.BlockSpec((2, FRESH_ROWS, block * LANES), lambda i: (0, 0, i)),
-        out_shape=jax.ShapeDtypeStruct((2, FRESH_ROWS, RANGE_BINS), jnp.bfloat16),
-        compiler_params=pltpu.CompilerParams(
-            dimension_semantics=("arbitrary",), vmem_limit_bytes=60 * MIB
-        ),
+        in_specs=[in_hbm(), in_hbm()],
+        out_specs=in_hbm(),
+        out_shape=jax.ShapeDtypeStruct(shape, jnp.bfloat16),
+        scratch_shapes=[
+            part,
+            part,
+            pltpu.VMEM(shape, jnp.bfloat16),
+            pltpu.SemaphoreType.DMA((PARTS,)),
+            pltpu.SemaphoreType.DMA((PARTS,)),
+            pltpu.SemaphoreType.DMA((PARTS,)),
+        ],
+        compiler_params=pltpu.CompilerParams(vmem_limit_bytes=60 * MIB),
         cost_estimate=pl.CostEstimate(
             flops=4 * FRESH_ROWS * RANGE_BINS, bytes_accessed=6 * MIB, transcendentals=0
         ),
@@ -604,14 +768,14 @@
     got = exchanged(range_compress(slab_echoes, fresh_pulses, range_filter))
     taps = migration_taps.reshape(BAND_MAX, PULSE_INNER, PULSE_OUTER)
     taps = taps.transpose(2, 1, 0).reshape(PULSES, BAND_MAX)
-    filt, taps = prepare(azimuth_filter, taps)
+    filt, narrow, taps = prepare(azimuth_filter, taps)
     bands = jnp.stack([band_offsets, band_widths]).reshape(2, 2, 1, HALF)
-    bands = jnp.broadcast_to(bands, (2, 2, 2, HALF)).reshape(2, 2, LANES)
+    bands = jnp.broadcast_to(bands, (2, 2, 2, HALF)).reshape(4, LANES)
     spectra0 = azimuth_forward(got, filt, 0)
     rim = from_next(spectra0)
-    spectra1 = azimuth_forward(got, filt, 1)
-    done0 = exchanged(azimuth_inverse(spectra0, spectra1, taps, bands[:, 0]))
-    done1 = exchanged(azimuth_inverse(spectra1, rim, taps, bands[:, 1]))
+    spectra1, ready0 = forward_and_inverse(got, filt, 1, spectra0, narrow, taps, bands)
+    done0 = exchanged(ready0)
+    done1 = exchanged(azimuth_inverse(spectra1, rim, narrow, taps, bands))
     return assemble(done0, done1)
 
 

time: 182 us -> 172 us (0.945)
  Pallas kernels: 93.3 us -> 77 us
  waiting for transfers between devices: 30.8 us -> 37.6 us
    pallas_call x2 -> x1, Pallas kernels: 16.1 us -> 7.86 us  [azimuth_forward(): pl.pallas_call(functools.partial(forward_kernel, half), in_specs=[in_hbm(...]
    all_to_all x2, waiting for transfers between devices: 30.8 us -> 37.6 us  [exchanged(): return lax.all_to_all(blocks, AXES, split_axis=0, concat_axis=0, tiled=True)]
    pallas_call x3, Pallas kernels: 41.2 us -> 37.2 us  [the longest x1 18.8 us: forward_and_inverse(): pl.pallas_call(functools.partial(middle_kernel, half), in_specs=[in_hbm()...]
    pallas_call x1, Pallas kernels: 23.1 us -> 19.7 us  [prepare(): pl.pallas_call(prepare_kernel, grid=(PULSE_OUTER // STEP,), in_specs=[pl....]
  transfers between devices with their start and end apart: 3 -> 3, of which waited for: 2 -> 2; matrix products, arithmetic and copies ran while one was open for 3% -> 3% of each run, Pallas kernels for 37% -> 31%
where the time goes in v3:
time: 172 us
  Pallas kernels  77 us (45%)
  waiting for transfers between devices  37.6 us (22%)
  blocking collectives  29.9 us (17%)
  starting transfers between devices  21.5 us (12%)
  local copies, waits for them, and re-layouts  5.51 us (3%)
    all_to_all x2, waiting for transfers between devices, exchanged(): return lax.all_to_all(blocks, AXES, split_axis=0, concat_axis=0, tiled=True)  37.6 us
    all_to_all x1, blocking collectives, exchanged(): return lax.all_to_all(blocks, AXES, split_axis=0, concat_axis=0, tiled=True)  29.9 us
    pallas_call x1, Pallas kernels, prepare(): pl.pallas_call(prepare_kernel, grid=(PULSE_OUTER // STEP,), in_specs=[pl....  19.7 us
    pallas_call x1, Pallas kernels, forward_and_inverse(): pl.pallas_call(functools.partial(middle_kernel, half), in_specs=[in_hbm()...  18.8 us
    all_to_all x2, starting transfers between devices, exchanged(): return lax.all_to_all(blocks, AXES, split_axis=0, concat_axis=0, tiled=True)  18.4 us
    pallas_call x1, Pallas kernels, azimuth_inverse(): pl.pallas_call(inverse_kernel, in_specs=[in_hbm()] * 4 + [in_vmem(), in_h...  14.7 us
    pallas_call x1, Pallas kernels, range_compress(): pl.pallas_call(range_kernel, grid=(ROWS // STEP,), in_specs=[whole((2, ST...  12.3 us
    pallas_call x1, Pallas kernels, azimuth_forward(): pl.pallas_call(functools.partial(forward_kernel, half), in_specs=[in_hbm(...  7.86 us
  transfers between devices with their start and end apart: 3, of which 2 were waited for; matrix products, arithmetic and copies ran while one was open for 3% of the time, Pallas kernels for 31%

profile of v3, /device:TPU:1, one launch (start us, length us, event | category | flops | bytes accessed | tf_op | source)
XLA Modules:
  0.0 171.7 jit_solution(11343760039124570720)
XLA Ops:
  0.0 12.3 %range_compress.1 = bf16[128,2,64,128]{3,2,1,0:T(8,128)(2,1)} custom-call(bf16[2,16,16384]{2,1,0:T(8,128)(2,1)} %slab.1, bf16[2,48,16384]{2,1,0:T(8,128)(2,1)} %fresh.1, f32[2,16384]{1,0:T(2,128)} %filt.1, bf16[256,256]{1,0:T(8,128)(2,1)} %constant.16.clone.t1.t3, bf16[256,256]{1,0:T(8,128)(2,1)} %constant.17.clone.t2.t4, ...), custom_call_target="tpu_custom_call" | custom-call | flops 4294967296 | bytes 8388608 | tf_op jit(solution)/shard_map/range_compress/pallas_call | solution.py:221
  12.3 0.0 copy-start.1
  12.3 12.0 %all-to-all-start = ((bf16[128,2,64,128]{3,2,1,0:T(8,128)(2,1)}), bf16[128,2,64,128]{3,2,1,0:T(8,128)(2,1)}, u32[]{:S(2)}, u32[]{:S(2)}) async-start(bf16[128,2,64,128]{3,2,1,0:T(8,128)(2,1)} %range_compress.1), calls=%async_computation | async-start | bytes 8388608 | tf_op jit(solution)/shard_map/all_to_all | solution.py:751
  24.2 0.0 copy-done.1
  24.2 0.1 copy.23
  24.4 4.5 %copy.22 = f32[9,64,128]{0,1,2:T(8,128)} copy(f32[9,64,128]{2,1,0:T(8,128)S(1)} %slice) | data formatting | bytes 589824 | tf_op jit(solution)/shard_map/reshape | solution.py:769
  28.9 19.7 %prepare.1 = (bf16[2,2,8192,128]{3,2,1,0:T(8,128)(2,1)}, bf16[8192,128]{1,0:T(8,128)(2,1)}, bf16[6,8192,128]{2,1,0:T(8,128)(2,1)}) custom-call(bf16[2,64,128,128]{3,2,1,0:T(8,128)(2,1)} %bitcast.10, f32[8192,9]{1,0:T(8,128)} %bitcast.9), custom_call_target="tpu_custom_call" | custom-call | flops 8388608 | bytes 35651584 | tf_op jit(solution)/shard_map/prepare/pallas_call | solution.py:282
  48.6 27.6 %all-to-all-done.got_hbm = bf16[128,2,64,128]{3,2,1,0:T(8,128)(2,1)} async-done(((bf16[128,2,64,128]{3,2,1,0:T(8,128)(2,1)}), bf16[128,2,64,128]{3,2,1,0:T(8,128)(2,1)}, u32[]{:S(2)}, u32[]{:S(2)}) %all-to-all-start) | async-done | bytes 4194336 | tf_op jit(solution)/shard_map/all_to_all | solution.py:751
  76.2 0.0 copy-start.2
  76.2 0.0 copy-start.3
  76.2 7.9 %azimuth_forward.1.left_hbm = bf16[8192,128]{1,0:T(8,128)(2,1)} custom-call(bf16[128,2,64,128]{3,2,1,0:T(8,128)(2,1)} %all-to-all-done.got_hbm, bf16[64,128,256]{2,1,0:T(8,128)(2,1)} %constant.20.clone.g1_hbm.f1_hbm, bf16[128,128]{1,0:T(8,128)(2,1)} %constant.21.clone.t2.f2, bf16[2,2,8192,128]{3,2,1,0:T(8,128)(2,1)} %get-tuple-element.10.filt_hbm), custom_call_target="tpu_custom_call" | custom-call | flops 1073741824 | bytes 12582912 | tf_op jit(solution)/shard_map/azimuth_forward/pallas_call | solution.py:400
  84.0 3.1 %collective-permute-start = (bf16[8192,128]{1,0:T(8,128)(2,1)}, bf16[8192,128]{1,0:T(8,128)(2,1)}, u32[]{:S(2)}, u32[]{:S(2)}) collective-permute-start(bf16[8192,128]{1,0:T(8,128)(2,1)} %azimuth_forward.1.left_hbm), channel_id=1, source_target_pairs={{1,0},{2,1},{3,2},{4,3},{5,4},{6,5},{7,6},{8,7},{9,8},{10,9},{11,1... | collective-permute-start | bytes 6291464 | tf_op jit(solution)/shard_map/ppermute | solution.py:756
  87.2 0.0 copy-done.2
  87.2 0.1 stack.9
  87.3 0.0 copy-done.3
  87.3 0.1 stack.10
  87.4 0.7 reshape.20.bands
  88.0 18.8 %forward_inverse.1 = (bf16[8192,128]{1,0:T(8,128)(2,1)}, bf16[128,48,128]{2,1,0:T(8,128)(2,1)}) custom-call(bf16[128,2,64,128]{3,2,1,0:T(8,128)(2,1)} %all-to-all-done.got_hbm, bf16[64,128,256]{2,1,0:T(8,128)(2,1)} %constant.20.clone.g1_hbm.f1_hbm, bf16[128,128]{1,0:T(8,128)(2,1)} %constant.21.clone.t2.f2, ...), custom_call_target="tpu_custom_call" | custom-call | flops 6979321856 | bytes 41943040 | tf_op jit(solution)/shard_map/forward_inverse/pallas_call | solution.py:629
  106.9 6.4 %all-to-all-start.1 = ((bf16[128,48,128]{2,1,0:T(8,128)(2,1)}), bf16[128,48,128]{2,1,0:T(8,128)(2,1)S(1)}, u32[]{:S(2)}, u32[]{:S(2)}) async-start(bf16[128,48,128]{2,1,0:T(8,128)(2,1)} %get-tuple-element.13), calls=%async_computation.1 | async-start | bytes 3145728 | tf_op jit(solution)/shard_map/all_to_all | solution.py:751
  113.3 0.0 collective-permute-done.right_hbm
  113.3 14.7 %migrate_inverse.1 = bf16[128,48,128]{2,1,0:T(8,128)(2,1)} custom-call(bf16[8192,128]{1,0:T(8,128)(2,1)} %get-tuple-element.14.left_hbm, bf16[8192,128]{1,0:T(8,128)(2,1)} %collective-permute-done.right_hbm, bf16[8192,128]{1,0:T(8,128)(2,1)} %get-tuple-element.11.narrow_hbm, bf16[6,8192,128]{2,1,0:T(8,128)(2,1)} %get-tuple-element.12.taps_hbm, ...), custom_call_target="tpu_custom_call" | custom-call | flops 5905580032 | bytes 12582912 | tf_op jit(solution)/shard_map/migrate_inverse/pallas_call | solution.py:670
  128.0 10.0 %all-to-all-done.1.first_hbm = bf16[128,48,128]{2,1,0:T(8,128)(2,1)S(1)} async-done(((bf16[128,48,128]{2,1,0:T(8,128)(2,1)}), bf16[128,48,128]{2,1,0:T(8,128)(2,1)S(1)}, u32[]{:S(2)}, u32[]{:S(2)}) %all-to-all-start.1) | async-done | bytes 1572896 | tf_op jit(solution)/shard_map/all_to_all | solution.py:751
  138.0 0.0 copy-start
  138.1 29.9 %all_to_all.15.second_hbm = bf16[128,48,128]{2,1,0:T(8,128)(2,1)} all-to-all(bf16[128,48,128]{2,1,0:T(8,128)(2,1)} %migrate_inverse.1), channel_id=1, replica_groups=mesh['az'=8,'rg'=16] {'az','rg'}, dimensions={0} | all-to-all | bytes 3145728 | tf_op jit(solution)/shard_map/all_to_all | solution.py:751
  167.9 0.0 copy-done
  167.9 3.6 %assemble.1 = bf16[2,48,16384]{2,1,0:T(8,128)(2,1)} custom-call(bf16[128,48,128]{2,1,0:T(8,128)(2,1)} %copy-done, bf16[128,48,128]{2,1,0:T(8,128)(2,1)} %all_to_all.15.second_hbm), custom_call_target="tpu_custom_call" | custom-call | flops 3145728 | bytes 6291456 | tf_op jit(solution)/shard_map/assemble/pallas_call | solution.py:729
  (3 shorter events, 0.0 us)
Async XLA Ops:
  12.3 12.0 %copy-start.1 = (f32[9,8192]{1,0:T(8,128)S(1)}, f32[9,8192]{1,0:T(8,128)}, u32[]{:S(2)}) copy-start(f32[9,8192]{1,0:T(8,128)} %param.25) | copy-start | bytes 884740
  12.3 63.9 %all-to-all-start = ((bf16[128,2,64,128]{3,2,1,0:T(8,128)(2,1)}), bf16[128,2,64,128]{3,2,1,0:T(8,128)(2,1)}, u32[]{:S(2)}, u32[]{:S(2)}) async-start(bf16[128,2,64,128]{3,2,1,0:T(8,128)(2,1)} %range_compress.1), calls=%async_computation | async-start | bytes 8388608 | tf_op jit(solution)/shard_map/all_to_all | solution.py:751
  76.2 11.0 %copy-start.2 = (s32[128]{0:T(128)S(1)}, s32[128]{0:T(128)}, u32[]{:S(2)}) copy-start(s32[128]{0:T(128)} %param.26) | copy-start | bytes 1540
  76.2 11.1 %copy-start.3 = (s32[128]{0:T(128)S(1)}, s32[128]{0:T(128)}, u32[]{:S(2)}) copy-start(s32[128]{0:T(128)} %param.27) | copy-start | bytes 1540
  84.0 29.2 %collective-permute-start = (bf16[8192,128]{1,0:T(8,128)(2,1)}, bf16[8192,128]{1,0:T(8,128)(2,1)}, u32[]{:S(2)}, u32[]{:S(2)}) collective-permute-start(bf16[8192,128]{1,0:T(8,128)(2,1)} %azimuth_forward.1.left_hbm), channel_id=1, source_target_pairs={{1,0},{2,1},{3,2},{4,3},{5,4},{6,5},{7,6},{8,7},{9,8},{10,9},{11,1... | collective-permute-start | bytes 6291464 | tf_op jit(solution)/shard_map/ppermute | solution.py:756
  106.9 31.2 %all-to-all-start.1 = ((bf16[128,48,128]{2,1,0:T(8,128)(2,1)}), bf16[128,48,128]{2,1,0:T(8,128)(2,1)S(1)}, u32[]{:S(2)}, u32[]{:S(2)}) async-start(bf16[128,48,128]{2,1,0:T(8,128)(2,1)} %get-tuple-element.13), calls=%async_computation.1 | async-start | bytes 3145728 | tf_op jit(solution)/shard_map/all_to_all | solution.py:751
  138.0 29.9 %copy-start = (bf16[128,48,128]{2,1,0:T(8,128)(2,1)}, bf16[128,48,128]{2,1,0:T(8,128)(2,1)S(1)}, u32[]{:S(2)}) copy-start(bf16[128,48,128]{2,1,0:T(8,128)(2,1)S(1)} %all-to-all-done.1.first_hbm) | copy-start | bytes 4718596

commit v4 on v3

--- a/solution.py
+++ b/solution.py
@@ -33,6 +33,7 @@
 PITCH = STEP + 4
 INNER_PITCH = PULSE_INNER + 8
 OUTER_PITCH = PULSE_OUTER + 8
+SPARE = 128
 BLOCKS = ROWS // STEP
 RANGE_LIMIT = 60
 FWD_LIMIT = 60
@@ -235,8 +236,8 @@
         out_specs=pl.BlockSpec((DEVICES, 2, STEP, LANES), lambda i: (0, 0, i, 0)),
         out_shape=out,
         scratch_shapes=[
-            pltpu.VMEM((2, RANGE_OUTER * PITCH, LANES), jnp.float32),
-            pltpu.VMEM((2, RANGE_OUTER * PITCH, LANES), jnp.float32),
+            pltpu.VMEM((2, RANGE_OUTER * PITCH + SPARE, LANES), jnp.float32),
+            pltpu.VMEM((2, RANGE_OUTER * PITCH + SPARE, LANES), jnp.float32),
             pltpu.VMEM((4, LANES, LANES), jnp.float32),
             pltpu.VMEM((STEP * LANES, 2 * LANES), jnp.bfloat16),
             pltpu.VMEM((STEP * LANES, 2 * LANES), jnp.bfloat16),
@@ -296,7 +297,7 @@
             jax.ShapeDtypeStruct((PULSES, LANES), jnp.bfloat16),
             jax.ShapeDtypeStruct((SPREAD, PULSES, LANES), jnp.bfloat16),
         ],
-        scratch_shapes=[pltpu.VMEM((2, PULSE_INNER * PITCH, LANES), jnp.float32)],
+        scratch_shapes=[pltpu.VMEM((2, PULSE_INNER * PITCH + SPARE, LANES), jnp.float32)],
         compiler_params=pltpu.CompilerParams(
             dimension_semantics=("arbitrary",), vmem_limit_bytes=60 * MIB
         ),
@@ -349,7 +350,7 @@
         return 0
 
     waits[1]()
-    lax.fori_loop(0, PULSE_INNER, outer, 0, unroll=16)
+    lax.fori_loop(0, PULSE_INNER, outer, 0, unroll=64)
 
     def inner(i, _):
         sides = []
@@ -407,8 +408,8 @@
             pltpu.VMEM(g1.shape, jnp.bfloat16),
             pltpu.VMEM((2, PULSES, LANES), jnp.bfloat16),
             pltpu.VMEM((PULSES, LANES), jnp.bfloat16),
-            pltpu.VMEM((PULSE_OUTER * INNER_PITCH, LANES), jnp.float32),
-            pltpu.VMEM((PULSE_OUTER * INNER_PITCH, LANES), jnp.float32),
+            pltpu.VMEM((PULSE_OUTER * INNER_PITCH + SPARE, LANES), jnp.float32),
+            pltpu.VMEM((PULSE_OUTER * INNER_PITCH + SPARE, LANES), jnp.float32),
             pltpu.SemaphoreType.DMA((3,)),
             pltpu.SemaphoreType.DMA((PARTS,)),
         ],
@@ -430,14 +431,21 @@
     return [(narrow_hbm, narrow)] + [(taps_hbm.at[at], taps.at[at]) for at in spans]
 
 
-def select_table(half, bands, sel):
+def own_half(half, row):
+    values = jnp.broadcast_to(row[...], (8, LANES))
+    here = (lane_ids(8) < HALF) == (half == 0)
+    return jnp.where(here, values, roll_half(values))[0:1]
+
+
+def select_table(half, offsets, widths, sel):
+    offsets, widths = own_half(half, offsets), own_half(half, widths)
     index = lax.broadcasted_iota(jnp.int32, (2 * LANES, LANES), 0)
     lane = lax.broadcasted_iota(jnp.int32, (2 * LANES, LANES), 1)
     column = jnp.where(index >= LANES, HALF, 0) + (index & (HALF - 1))
     same = ((index >> 6) & 1) == (lane >> 6)
-    want = (lane & (HALF - 1)) + bands[half : half + 1, :]
+    want = (lane & (HALF - 1)) + offsets
     for j in range(BAND_MAX):
-        hit = same & (column == want + j) & (bands[2 + half : 3 + half, :] > j)
+        hit = same & (column == want + j) & (widths > j)
         sel[:, j * LANES : (j + 1) * LANES] = jnp.where(hit, 1.0, 0.0).astype(jnp.bfloat16)
 
 
@@ -482,7 +490,7 @@
         return 0
 
     waits[-1]()
-    lax.fori_loop(0, PULSE_OUTER, inner, 0, unroll=32)
+    lax.fori_loop(0, PULSE_OUTER, inner, 0, unroll=64)
 
     def last(i, _):
         sides = []
@@ -499,7 +507,7 @@
             ]
         return 0
 
-    lax.fori_loop(0, PULSE_INNER // 2, last, 0, unroll=8)
+    lax.fori_loop(0, PULSE_INNER // 2, last, 0, unroll=32)
 
     quarter = PULSE_INNER // STEP
     fresh_units = FRESH_ROWS // STEP
@@ -523,7 +531,8 @@
     right_hbm,
     narrow_hbm,
     taps_hbm,
-    bands,
+    offsets,
+    widths,
     g1_hbm,
     t2,
     out_hbm,
@@ -543,7 +552,7 @@
 ):
     pairs = [(left_hbm, left), (right_hbm, right), *tap_pairs(narrow_hbm, narrow, taps_hbm, taps), (g1_hbm, g1)]
     copies = start_all(pairs, sems)
-    select_table(1, bands, sel)
+    select_table(1, offsets, widths, sel)
 
     def both():
         copies[0].wait()
@@ -564,7 +573,8 @@
     left_hbm,
     narrow_hbm,
     taps_hbm,
-    bands,
+    offsets,
+    widths,
     g1_hbm,
     t2,
     right_hbm,
@@ -592,7 +602,7 @@
     first.append(pltpu.make_async_copy(filt_hbm.at[half], filt, sems.at[2]))
     pairs = [(left_hbm, left), *tap_pairs(narrow_hbm, narrow, taps_hbm, taps), (g1_hbm, g1)]
     late = [pltpu.make_async_copy(a, b, late_sems.at[i]) for i, (a, b) in enumerate(pairs)]
-    select_table(0, bands, sel)
+    select_table(0, offsets, widths, sel)
 
     cut = 4
     waits = [
@@ -601,7 +611,7 @@
         then_start(first[2], late[cut:]),
     ]
     inner = forward_steps(got, f1, f2, filt, right, ps, ts, waits)
-    lax.fori_loop(0, PULSE_OUTER // 2, inner, 0, unroll=16)
+    lax.fori_loop(0, PULSE_OUTER // 2, inner, 0, unroll=64)
     put_right = pltpu.make_async_copy(right, right_hbm, right_sem.at[0])
     put_right.start()
     waits = [copy.wait for copy in late]
@@ -629,7 +639,7 @@
     return pl.pallas_call(
         functools.partial(middle_kernel, half),
         in_specs=[in_hbm(), in_hbm(), in_vmem()] + [in_hbm()] * 4
-        + [in_vmem(), in_hbm(), in_vmem()],
+        + [in_vmem(), in_vmem(), in_hbm(), in_vmem()],
         out_specs=[in_hbm(), in_hbm()],
         out_shape=[
             jax.ShapeDtypeStruct((PULSES, LANES), jnp.bfloat16),
@@ -640,8 +650,8 @@
             pltpu.VMEM(f1.shape, jnp.bfloat16),
             pltpu.VMEM((2, PULSES, LANES), jnp.bfloat16),
             pltpu.VMEM((PULSES, LANES), jnp.bfloat16),
-            pltpu.VMEM((PULSE_OUTER * INNER_PITCH, LANES), jnp.float32),
-            pltpu.VMEM((PULSE_OUTER * INNER_PITCH, LANES), jnp.float32),
+            pltpu.VMEM((PULSE_OUTER * INNER_PITCH + SPARE, LANES), jnp.float32),
+            pltpu.VMEM((PULSE_OUTER * INNER_PITCH + SPARE, LANES), jnp.float32),
             pltpu.VMEM((PULSES, LANES), jnp.bfloat16),
             pltpu.VMEM((PULSES, LANES), jnp.bfloat16),
             pltpu.VMEM((SPREAD, PULSES, LANES), jnp.bfloat16),
@@ -662,14 +672,14 @@
             transcendentals=0,
         ),
         name="forward_inverse",
-    )(got, f1, f2, filt, left, narrow, taps, bands, g1, t2)
+    )(got, f1, f2, filt, left, narrow, taps, *bands, g1, t2)
 
 
 def azimuth_inverse(left, right, narrow, taps, bands):
     g1, t2 = inverse_tables()
     return pl.pallas_call(
         inverse_kernel,
-        in_specs=[in_hbm()] * 4 + [in_vmem(), in_hbm(), in_vmem()],
+        in_specs=[in_hbm()] * 4 + [in_vmem(), in_vmem(), in_hbm(), in_vmem()],
         out_specs=in_hbm(),
         out_shape=jax.ShapeDtypeStruct((DEVICES, FRESH_ROWS, LANES), jnp.bfloat16),
         scratch_shapes=[
@@ -682,8 +692,8 @@
             pltpu.VMEM((2 * LANES, BAND_MAX * LANES), jnp.bfloat16),
             pltpu.VMEM((PULSES, LANES), jnp.float32),
             pltpu.VMEM((PULSES, LANES), jnp.bfloat16),
-            pltpu.VMEM((PULSE_INNER * OUTER_PITCH, LANES), jnp.float32),
-            pltpu.VMEM((KEPT_OUTER * INNER_PITCH, LANES), jnp.float32),
+            pltpu.VMEM((PULSE_INNER * OUTER_PITCH + SPARE, LANES), jnp.float32),
+            pltpu.VMEM((KEPT_OUTER * INNER_PITCH + SPARE, LANES), jnp.float32),
             pltpu.SemaphoreType.DMA((4 + SPREAD // 2,)),
             pltpu.SemaphoreType.DMA((PARTS,)),
         ],
@@ -694,7 +704,7 @@
             transcendentals=0,
         ),
         name="migrate_inverse",
-    )(left, right, narrow, taps, bands, g1, t2)
+    )(left, right, narrow, taps, *bands, g1, t2)
 
 
 def assemble_kernel(first_hbm, second_hbm, out_hbm, first, second, out, sems, more_sems, out_sems):
@@ -769,8 +779,7 @@
     taps = migration_taps.reshape(BAND_MAX, PULSE_INNER, PULSE_OUTER)
     taps = taps.transpose(2, 1, 0).reshape(PULSES, BAND_MAX)
     filt, narrow, taps = prepare(azimuth_filter, taps)
-    bands = jnp.stack([band_offsets, band_widths]).reshape(2, 2, 1, HALF)
-    bands = jnp.broadcast_to(bands, (2, 2, 2, HALF)).reshape(4, LANES)
+    bands = (band_offsets.reshape(1, LANES), band_widths.reshape(1, LANES))
     spectra0 = azimuth_forward(got, filt, 0)
     rim = from_next(spectra0)
     spectra1, ready0 = forward_and_inverse(got, filt, 1, spectra0, narrow, taps, bands)

time: 172 us -> 169 us (0.983)
  Pallas kernels: 77 us -> 73.6 us
    ppermute x1, waiting for transfers between devices: 0.01 us -> 2.81 us  [from_next(): return lax.ppermute(block, AXES, [(i + 1, i) for i in range(size - 1)])]
    pallas_call x1, Pallas kernels: 18.8 us -> 16.8 us  [forward_and_inverse(): pl.pallas_call(functools.partial(middle_kernel, half), in_specs=[in_hbm()...]
    all_to_all x2, waiting for transfers between devices: 37.6 us -> 35.8 us  [exchanged(): return lax.all_to_all(blocks, AXES, split_axis=0, concat_axis=0, tiled=True)]
  transfers between devices with their start and end apart: 3 -> 3, of which waited for: 2 -> 3; matrix products, arithmetic and copies ran while one was open for 3% -> 3% of each run, Pallas kernels for 31% -> 30%
where the time goes in v4:
time: 169 us; the launch traced here: 168 us
  Pallas kernels  73.6 us (44%)
  waiting for transfers between devices  38.6 us (23%)
  blocking collectives  29.9 us (18%)
  starting transfers between devices  21.5 us (13%)
  local copies, waits for them, and re-layouts  4.65 us (3%)
    all_to_all x2, waiting for transfers between devices, exchanged(): return lax.all_to_all(blocks, AXES, split_axis=0, concat_axis=0, tiled=True)  35.8 us
    all_to_all x1, blocking collectives, exchanged(): return lax.all_to_all(blocks, AXES, split_axis=0, concat_axis=0, tiled=True)  29.9 us
    pallas_call x1, Pallas kernels, prepare(): pl.pallas_call(prepare_kernel, grid=(PULSE_OUTER // STEP,), in_specs=[pl....  19.7 us
    all_to_all x2, starting transfers between devices, exchanged(): return lax.all_to_all(blocks, AXES, split_axis=0, concat_axis=0, tiled=True)  18.3 us
    pallas_call x1, Pallas kernels, forward_and_inverse(): pl.pallas_call(functools.partial(middle_kernel, half), in_specs=[in_hbm()...  16.8 us
    pallas_call x1, Pallas kernels, azimuth_inverse(): pl.pallas_call(inverse_kernel, in_specs=[in_hbm()] * 4 + [in_vmem(), in_v...  13.8 us
    pallas_call x1, Pallas kernels, range_compress(): pl.pallas_call(range_kernel, grid=(ROWS // STEP,), in_specs=[whole((2, ST...  12.3 us
    pallas_call x1, Pallas kernels, azimuth_forward(): pl.pallas_call(functools.partial(forward_kernel, half), in_specs=[in_hbm(...  7.44 us
  transfers between devices with their start and end apart: 3, of which 3 were waited for; matrix products, arithmetic and copies ran while one was open for 3% of the time, Pallas kernels for 30%

profile of v4, /device:TPU:1, one launch (start us, length us, event | category | flops | bytes accessed | tf_op | source)
XLA Modules:
  0.0 168.4 jit_solution(7648918421980536330)
XLA Ops:
  0.0 12.3 %range_compress.1 = bf16[128,2,64,128]{3,2,1,0:T(8,128)(2,1)} custom-call(bf16[2,16,16384]{2,1,0:T(8,128)(2,1)} %slab.1, bf16[2,48,16384]{2,1,0:T(8,128)(2,1)} %fresh.1, f32[2,16384]{1,0:T(2,128)} %filt.1, bf16[256,256]{1,0:T(8,128)(2,1)} %constant.16.clone.t1.t3, bf16[256,256]{1,0:T(8,128)(2,1)} %constant.17.clone.t2.t4, ...), custom_call_target="tpu_custom_call" | custom-call | flops 4294967296 | bytes 8388608 | tf_op jit(solution)/shard_map/range_compress/pallas_call | solution.py:222
  12.3 0.0 copy-start.1
  12.3 12.0 %all-to-all-start = ((bf16[128,2,64,128]{3,2,1,0:T(8,128)(2,1)}), bf16[128,2,64,128]{3,2,1,0:T(8,128)(2,1)}, u32[]{:S(2)}, u32[]{:S(2)}) async-start(bf16[128,2,64,128]{3,2,1,0:T(8,128)(2,1)} %range_compress.1), calls=%async_computation | async-start | bytes 8388608 | tf_op jit(solution)/shard_map/all_to_all | solution.py:761
  24.2 0.0 copy-done.1
  24.2 0.1 copy.23
  24.4 4.5 %copy.22 = f32[9,64,128]{0,1,2:T(8,128)} copy(f32[9,64,128]{2,1,0:T(8,128)S(1)} %slice) | data formatting | bytes 589824 | tf_op jit(solution)/shard_map/reshape | solution.py:779
  28.9 19.7 %prepare.1 = (bf16[2,2,8192,128]{3,2,1,0:T(8,128)(2,1)}, bf16[8192,128]{1,0:T(8,128)(2,1)}, bf16[6,8192,128]{2,1,0:T(8,128)(2,1)}) custom-call(bf16[2,64,128,128]{3,2,1,0:T(8,128)(2,1)} %bitcast.10, f32[8192,9]{1,0:T(8,128)} %bitcast.9), custom_call_target="tpu_custom_call" | custom-call | flops 8388608 | bytes 35651584 | tf_op jit(solution)/shard_map/prepare/pallas_call | solution.py:283
  48.5 27.6 %all-to-all-done.got_hbm = bf16[128,2,64,128]{3,2,1,0:T(8,128)(2,1)} async-done(((bf16[128,2,64,128]{3,2,1,0:T(8,128)(2,1)}), bf16[128,2,64,128]{3,2,1,0:T(8,128)(2,1)}, u32[]{:S(2)}, u32[]{:S(2)}) %all-to-all-start) | async-done | bytes 4194336 | tf_op jit(solution)/shard_map/all_to_all | solution.py:761
  76.2 7.4 %azimuth_forward.1.left_hbm = bf16[8192,128]{1,0:T(8,128)(2,1)} custom-call(bf16[128,2,64,128]{3,2,1,0:T(8,128)(2,1)} %all-to-all-done.got_hbm, bf16[64,128,256]{2,1,0:T(8,128)(2,1)} %constant.20.clone.g1_hbm.f1_hbm, bf16[128,128]{1,0:T(8,128)(2,1)} %constant.21.clone.t2.f2, bf16[2,2,8192,128]{3,2,1,0:T(8,128)(2,1)} %get-tuple-element.10.filt_hbm), custom_call_target="tpu_custom_call" | custom-call | flops 1073741824 | bytes 12582912 | tf_op jit(solution)/shard_map/azimuth_forward/pallas_call | solution.py:401
  83.6 3.1 %collective-permute-start = (bf16[8192,128]{1,0:T(8,128)(2,1)}, bf16[8192,128]{1,0:T(8,128)(2,1)}, u32[]{:S(2)}, u32[]{:S(2)}) collective-permute-start(bf16[8192,128]{1,0:T(8,128)(2,1)} %azimuth_forward.1.left_hbm), channel_id=1, source_target_pairs={{1,0},{2,1},{3,2},{4,3},{5,4},{6,5},{7,6},{8,7},{9,8},{10,9},{11,1... | collective-permute-start | bytes 6291464 | tf_op jit(solution)/shard_map/ppermute | solution.py:766
  86.7 16.8 %forward_inverse.1 = (bf16[8192,128]{1,0:T(8,128)(2,1)}, bf16[128,48,128]{2,1,0:T(8,128)(2,1)}) custom-call(bf16[128,2,64,128]{3,2,1,0:T(8,128)(2,1)} %all-to-all-done.got_hbm, bf16[64,128,256]{2,1,0:T(8,128)(2,1)} %constant.20.clone.g1_hbm.f1_hbm, bf16[128,128]{1,0:T(8,128)(2,1)} %constant.21.clone.t2.f2, ...), custom_call_target="tpu_custom_call" | custom-call | flops 6979321856 | bytes 41943040 | tf_op jit(solution)/shard_map/forward_inverse/pallas_call | solution.py:639
  103.6 6.4 %all-to-all-start.1 = ((bf16[128,48,128]{2,1,0:T(8,128)(2,1)}), bf16[128,48,128]{2,1,0:T(8,128)(2,1)S(1)}, u32[]{:S(2)}, u32[]{:S(2)}) async-start(bf16[128,48,128]{2,1,0:T(8,128)(2,1)} %get-tuple-element.13), calls=%async_computation.1 | async-start | bytes 3145728 | tf_op jit(solution)/shard_map/all_to_all | solution.py:761
  110.0 2.8 %collective-permute-done.right_hbm = bf16[8192,128]{1,0:T(8,128)(2,1)} collective-permute-done((bf16[8192,128]{1,0:T(8,128)(2,1)}, bf16[8192,128]{1,0:T(8,128)(2,1)}, u32[]{:S(2)}, u32[]{:S(2)}) %collective-permute-start) | collective-permute-done | bytes 2097184 | tf_op jit(solution)/shard_map/ppermute | solution.py:766
  112.8 13.8 %migrate_inverse.1 = bf16[128,48,128]{2,1,0:T(8,128)(2,1)} custom-call(bf16[8192,128]{1,0:T(8,128)(2,1)} %get-tuple-element.14.left_hbm, bf16[8192,128]{1,0:T(8,128)(2,1)} %collective-permute-done.right_hbm, bf16[8192,128]{1,0:T(8,128)(2,1)} %get-tuple-element.11.narrow_hbm, bf16[6,8192,128]{2,1,0:T(8,128)(2,1)} %get-tuple-element.12.taps_hbm, ...), custom_call_target="tpu_custom_call" | custom-call | flops 5905580032 | bytes 12582912 | tf_op jit(solution)/shard_map/migrate_inverse/pallas_call | solution.py:680
  126.6 8.2 %all-to-all-done.1.first_hbm = bf16[128,48,128]{2,1,0:T(8,128)(2,1)S(1)} async-done(((bf16[128,48,128]{2,1,0:T(8,128)(2,1)}), bf16[128,48,128]{2,1,0:T(8,128)(2,1)S(1)}, u32[]{:S(2)}, u32[]{:S(2)}) %all-to-all-start.1) | async-done | bytes 1572896 | tf_op jit(solution)/shard_map/all_to_all | solution.py:761
  134.7 0.0 copy-start
  134.7 29.9 %all_to_all.15.second_hbm = bf16[128,48,128]{2,1,0:T(8,128)(2,1)} all-to-all(bf16[128,48,128]{2,1,0:T(8,128)(2,1)} %migrate_inverse.1), channel_id=1, replica_groups=mesh['az'=8,'rg'=16] {'az','rg'}, dimensions={0} | all-to-all | bytes 3145728 | tf_op jit(solution)/shard_map/all_to_all | solution.py:761
  164.6 0.0 copy-done
  164.6 3.6 %assemble.1 = bf16[2,48,16384]{2,1,0:T(8,128)(2,1)} custom-call(bf16[128,48,128]{2,1,0:T(8,128)(2,1)} %copy-done, bf16[128,48,128]{2,1,0:T(8,128)(2,1)} %all_to_all.15.second_hbm), custom_call_target="tpu_custom_call" | custom-call | flops 3145728 | bytes 6291456 | tf_op jit(solution)/shard_map/assemble/pallas_call | solution.py:739
  (1 shorter events, 0.0 us)
Async XLA Ops:
  12.3 12.0 %copy-start.1 = (f32[9,8192]{1,0:T(8,128)S(1)}, f32[9,8192]{1,0:T(8,128)}, u32[]{:S(2)}) copy-start(f32[9,8192]{1,0:T(8,128)} %param.25) | copy-start | bytes 884740
  12.3 63.9 %all-to-all-start = ((bf16[128,2,64,128]{3,2,1,0:T(8,128)(2,1)}), bf16[128,2,64,128]{3,2,1,0:T(8,128)(2,1)}, u32[]{:S(2)}, u32[]{:S(2)}) async-start(bf16[128,2,64,128]{3,2,1,0:T(8,128)(2,1)} %range_compress.1), calls=%async_computation | async-start | bytes 8388608 | tf_op jit(solution)/shard_map/all_to_all | solution.py:761
  83.6 29.2 %collective-permute-start = (bf16[8192,128]{1,0:T(8,128)(2,1)}, bf16[8192,128]{1,0:T(8,128)(2,1)}, u32[]{:S(2)}, u32[]{:S(2)}) collective-permute-start(bf16[8192,128]{1,0:T(8,128)(2,1)} %azimuth_forward.1.left_hbm), channel_id=1, source_target_pairs={{1,0},{2,1},{3,2},{4,3},{5,4},{6,5},{7,6},{8,7},{9,8},{10,9},{11,1... | collective-permute-start | bytes 6291464 | tf_op jit(solution)/shard_map/ppermute | solution.py:766
  103.6 31.2 %all-to-all-start.1 = ((bf16[128,48,128]{2,1,0:T(8,128)(2,1)}), bf16[128,48,128]{2,1,0:T(8,128)(2,1)S(1)}, u32[]{:S(2)}, u32[]{:S(2)}) async-start(bf16[128,48,128]{2,1,0:T(8,128)(2,1)} %get-tuple-element.13), calls=%async_computation.1 | async-start | bytes 3145728 | tf_op jit(solution)/shard_map/all_to_all | solution.py:761
  134.7 29.9 %copy-start = (bf16[128,48,128]{2,1,0:T(8,128)(2,1)}, bf16[128,48,128]{2,1,0:T(8,128)(2,1)S(1)}, u32[]{:S(2)}) copy-start(bf16[128,48,128]{2,1,0:T(8,128)(2,1)S(1)} %all-to-all-done.1.first_hbm) | copy-start | bytes 4718596

commit v5 on v4

--- a/solution.py
+++ b/solution.py
@@ -127,7 +127,7 @@
                 xs[c, to, :] = source[c, :, at].astype(jnp.float32)
             return 0
 
-        lax.fori_loop(0, RANGE_OUTER, one, 0, unroll=8)
+        lax.fori_loop(0, RANGE_OUTER, one, 0, unroll=32)
 
     @pl.when(step == 0)
     def _():
@@ -200,7 +200,7 @@
         out[n1, 1] = os[1, at, :].astype(jnp.bfloat16)
         return 0
 
-    lax.fori_loop(0, RANGE_OUTER, store, 0, unroll=8)
+    lax.fori_loop(0, RANGE_OUTER, store, 0, unroll=32)
 
 
 def whole(shape):
@@ -341,7 +341,7 @@
                 ps[pl.ds(at, STEP), :] = block[(k + 1) * STEP : (k + 2) * STEP]
         return 0
 
-    lax.fori_loop(0, DEVICES // quarter, unpack, 0, unroll=2)
+    lax.fori_loop(0, DEVICES // quarter, unpack, 0, unroll=8)
 
     def outer(l, _):
         x = ps[pl.ds(l, PULSE_OUTER, stride=INNER_PITCH), :]
@@ -725,7 +725,7 @@
     for i in range(PARTS):
         copies[i].wait()
         more[i].wait()
-        lax.fori_loop(i * size, (i + 1) * size, one, 0, unroll=16)
+        lax.fori_loop(i * size, (i + 1) * size, one, 0, unroll=32)
         at = pl.ds(i * size * LANES, size * LANES)
         puts.append(pltpu.make_async_copy(out.at[:, :, at], out_hbm.at[:, :, at], out_sems.at[i]))
         puts[i].start()

time: 169 us -> 168 us (level)
  no operation moved by 1% of the time
where the time goes in v5:
time: 168 us
  Pallas kernels  73 us (43%)
  waiting for transfers between devices  38.6 us (23%)
  blocking collectives  29.9 us (18%)
  starting transfers between devices  21.5 us (13%)
  local copies, waits for them, and re-layouts  4.65 us (3%)
    all_to_all x2, waiting for transfers between devices, exchanged(): return lax.all_to_all(blocks, AXES, split_axis=0, concat_axis=0, tiled=True)  35.8 us
    all_to_all x1, blocking collectives, exchanged(): return lax.all_to_all(blocks, AXES, split_axis=0, concat_axis=0, tiled=True)  29.9 us
    pallas_call x1, Pallas kernels, prepare(): pl.pallas_call(prepare_kernel, grid=(PULSE_OUTER // STEP,), in_specs=[pl....  19.7 us
    all_to_all x2, starting transfers between devices, exchanged(): return lax.all_to_all(blocks, AXES, split_axis=0, concat_axis=0, tiled=True)  18.3 us
    pallas_call x1, Pallas kernels, forward_and_inverse(): pl.pallas_call(functools.partial(middle_kernel, half), in_specs=[in_hbm()...  16.8 us
    pallas_call x1, Pallas kernels, azimuth_inverse(): pl.pallas_call(inverse_kernel, in_specs=[in_hbm()] * 4 + [in_vmem(), in_v...  13.8 us
    pallas_call x1, Pallas kernels, range_compress(): pl.pallas_call(range_kernel, grid=(ROWS // STEP,), in_specs=[whole((2, ST...  11.9 us
    pallas_call x1, Pallas kernels, azimuth_forward(): pl.pallas_call(functools.partial(forward_kernel, half), in_specs=[in_hbm(...  7.44 us
  transfers between devices with their start and end apart: 3, of which 3 were waited for; matrix products, arithmetic and copies ran while one was open for 3% of the time, Pallas kernels for 30%

profile of v5, /device:TPU:1, one launch (start us, length us, event | category | flops | bytes accessed | tf_op | source)
XLA Modules:
  0.0 167.8 jit_solution(9795984394230167015)
XLA Ops:
  0.0 11.9 %range_compress.1 = bf16[128,2,64,128]{3,2,1,0:T(8,128)(2,1)} custom-call(bf16[2,16,16384]{2,1,0:T(8,128)(2,1)} %slab.1, bf16[2,48,16384]{2,1,0:T(8,128)(2,1)} %fresh.1, f32[2,16384]{1,0:T(2,128)} %filt.1, bf16[256,256]{1,0:T(8,128)(2,1)} %constant.16.clone.t1.t3, bf16[256,256]{1,0:T(8,128)(2,1)} %constant.17.clone.t2.t4, ...), custom_call_target="tpu_custom_call" | custom-call | flops 4294967296 | bytes 8388608 | tf_op jit(solution)/shard_map/range_compress/pallas_call | solution.py:222
  11.9 0.0 copy-start.1
  11.9 12.0 %all-to-all-start = ((bf16[128,2,64,128]{3,2,1,0:T(8,128)(2,1)}), bf16[128,2,64,128]{3,2,1,0:T(8,128)(2,1)}, u32[]{:S(2)}, u32[]{:S(2)}) async-start(bf16[128,2,64,128]{3,2,1,0:T(8,128)(2,1)} %range_compress.1), calls=%async_computation | async-start | bytes 8388608 | tf_op jit(solution)/shard_map/all_to_all | solution.py:761
  23.8 0.0 copy-done.1
  23.8 0.1 copy.23
  24.0 4.5 %copy.22 = f32[9,64,128]{0,1,2:T(8,128)} copy(f32[9,64,128]{2,1,0:T(8,128)S(1)} %slice) | data formatting | bytes 589824 | tf_op jit(solution)/shard_map/reshape | solution.py:779
  28.5 19.7 %prepare.1 = (bf16[2,2,8192,128]{3,2,1,0:T(8,128)(2,1)}, bf16[8192,128]{1,0:T(8,128)(2,1)}, bf16[6,8192,128]{2,1,0:T(8,128)(2,1)}) custom-call(bf16[2,64,128,128]{3,2,1,0:T(8,128)(2,1)} %bitcast.10, f32[8192,9]{1,0:T(8,128)} %bitcast.9), custom_call_target="tpu_custom_call" | custom-call | flops 8388608 | bytes 35651584 | tf_op jit(solution)/shard_map/prepare/pallas_call | solution.py:283
  48.2 27.6 %all-to-all-done.got_hbm = bf16[128,2,64,128]{3,2,1,0:T(8,128)(2,1)} async-done(((bf16[128,2,64,128]{3,2,1,0:T(8,128)(2,1)}), bf16[128,2,64,128]{3,2,1,0:T(8,128)(2,1)}, u32[]{:S(2)}, u32[]{:S(2)}) %all-to-all-start) | async-done | bytes 4194336 | tf_op jit(solution)/shard_map/all_to_all | solution.py:761
  75.8 7.4 %azimuth_forward.1.left_hbm = bf16[8192,128]{1,0:T(8,128)(2,1)} custom-call(bf16[128,2,64,128]{3,2,1,0:T(8,128)(2,1)} %all-to-all-done.got_hbm, bf16[64,128,256]{2,1,0:T(8,128)(2,1)} %constant.20.clone.g1_hbm.f1_hbm, bf16[128,128]{1,0:T(8,128)(2,1)} %constant.21.clone.t2.f2, bf16[2,2,8192,128]{3,2,1,0:T(8,128)(2,1)} %get-tuple-element.10.filt_hbm), custom_call_target="tpu_custom_call" | custom-call | flops 1073741824 | bytes 12582912 | tf_op jit(solution)/shard_map/azimuth_forward/pallas_call | solution.py:401
  83.2 3.1 %collective-permute-start = (bf16[8192,128]{1,0:T(8,128)(2,1)}, bf16[8192,128]{1,0:T(8,128)(2,1)}, u32[]{:S(2)}, u32[]{:S(2)}) collective-permute-start(bf16[8192,128]{1,0:T(8,128)(2,1)} %azimuth_forward.1.left_hbm), channel_id=1, source_target_pairs={{1,0},{2,1},{3,2},{4,3},{5,4},{6,5},{7,6},{8,7},{9,8},{10,9},{11,1... | collective-permute-start | bytes 6291464 | tf_op jit(solution)/shard_map/ppermute | solution.py:766
  86.4 16.8 %forward_inverse.1 = (bf16[8192,128]{1,0:T(8,128)(2,1)}, bf16[128,48,128]{2,1,0:T(8,128)(2,1)}) custom-call(bf16[128,2,64,128]{3,2,1,0:T(8,128)(2,1)} %all-to-all-done.got_hbm, bf16[64,128,256]{2,1,0:T(8,128)(2,1)} %constant.20.clone.g1_hbm.f1_hbm, bf16[128,128]{1,0:T(8,128)(2,1)} %constant.21.clone.t2.f2, ...), custom_call_target="tpu_custom_call" | custom-call | flops 6979321856 | bytes 41943040 | tf_op jit(solution)/shard_map/forward_inverse/pallas_call | solution.py:639
  103.2 6.4 %all-to-all-start.1 = ((bf16[128,48,128]{2,1,0:T(8,128)(2,1)}), bf16[128,48,128]{2,1,0:T(8,128)(2,1)S(1)}, u32[]{:S(2)}, u32[]{:S(2)}) async-start(bf16[128,48,128]{2,1,0:T(8,128)(2,1)} %get-tuple-element.13), calls=%async_computation.1 | async-start | bytes 3145728 | tf_op jit(solution)/shard_map/all_to_all | solution.py:761
  109.6 2.8 %collective-permute-done.right_hbm = bf16[8192,128]{1,0:T(8,128)(2,1)} collective-permute-done((bf16[8192,128]{1,0:T(8,128)(2,1)}, bf16[8192,128]{1,0:T(8,128)(2,1)}, u32[]{:S(2)}, u32[]{:S(2)}) %collective-permute-start) | collective-permute-done | bytes 2097184 | tf_op jit(solution)/shard_map/ppermute | solution.py:766
  112.4 13.8 %migrate_inverse.1 = bf16[128,48,128]{2,1,0:T(8,128)(2,1)} custom-call(bf16[8192,128]{1,0:T(8,128)(2,1)} %get-tuple-element.14.left_hbm, bf16[8192,128]{1,0:T(8,128)(2,1)} %collective-permute-done.right_hbm, bf16[8192,128]{1,0:T(8,128)(2,1)} %get-tuple-element.11.narrow_hbm, bf16[6,8192,128]{2,1,0:T(8,128)(2,1)} %get-tuple-element.12.taps_hbm, ...), custom_call_target="tpu_custom_call" | custom-call | flops 5905580032 | bytes 12582912 | tf_op jit(solution)/shard_map/migrate_inverse/pallas_call | solution.py:680
  126.2 8.2 %all-to-all-done.1.first_hbm = bf16[128,48,128]{2,1,0:T(8,128)(2,1)S(1)} async-done(((bf16[128,48,128]{2,1,0:T(8,128)(2,1)}), bf16[128,48,128]{2,1,0:T(8,128)(2,1)S(1)}, u32[]{:S(2)}, u32[]{:S(2)}) %all-to-all-start.1) | async-done | bytes 1572896 | tf_op jit(solution)/shard_map/all_to_all | solution.py:761
  134.4 0.0 copy-start
  134.4 29.9 %all_to_all.15.second_hbm = bf16[128,48,128]{2,1,0:T(8,128)(2,1)} all-to-all(bf16[128,48,128]{2,1,0:T(8,128)(2,1)} %migrate_inverse.1), channel_id=1, replica_groups=mesh['az'=8,'rg'=16] {'az','rg'}, dimensions={0} | all-to-all | bytes 3145728 | tf_op jit(solution)/shard_map/all_to_all | solution.py:761
  164.2 0.0 copy-done
  164.2 3.4 %assemble.1 = bf16[2,48,16384]{2,1,0:T(8,128)(2,1)} custom-call(bf16[128,48,128]{2,1,0:T(8,128)(2,1)} %copy-done, bf16[128,48,128]{2,1,0:T(8,128)(2,1)} %all_to_all.15.second_hbm), custom_call_target="tpu_custom_call" | custom-call | flops 3145728 | bytes 6291456 | tf_op jit(solution)/shard_map/assemble/pallas_call | solution.py:739
  (1 shorter events, 0.0 us)
Async XLA Ops:
  11.9 12.0 %copy-start.1 = (f32[9,8192]{1,0:T(8,128)S(1)}, f32[9,8192]{1,0:T(8,128)}, u32[]{:S(2)}) copy-start(f32[9,8192]{1,0:T(8,128)} %param.25) | copy-start | bytes 884740
  11.9 63.9 %all-to-all-start = ((bf16[128,2,64,128]{3,2,1,0:T(8,128)(2,1)}), bf16[128,2,64,128]{3,2,1,0:T(8,128)(2,1)}, u32[]{:S(2)}, u32[]{:S(2)}) async-start(bf16[128,2,64,128]{3,2,1,0:T(8,128)(2,1)} %range_compress.1), calls=%async_computation | async-start | bytes 8388608 | tf_op jit(solution)/shard_map/all_to_all | solution.py:761
  83.2 29.2 %collective-permute-start = (bf16[8192,128]{1,0:T(8,128)(2,1)}, bf16[8192,128]{1,0:T(8,128)(2,1)}, u32[]{:S(2)}, u32[]{:S(2)}) collective-permute-start(bf16[8192,128]{1,0:T(8,128)(2,1)} %azimuth_forward.1.left_hbm), channel_id=1, source_target_pairs={{1,0},{2,1},{3,2},{4,3},{5,4},{6,5},{7,6},{8,7},{9,8},{10,9},{11,1... | collective-permute-start | bytes 6291464 | tf_op jit(solution)/shard_map/ppermute | solution.py:766
  103.2 31.2 %all-to-all-start.1 = ((bf16[128,48,128]{2,1,0:T(8,128)(2,1)}), bf16[128,48,128]{2,1,0:T(8,128)(2,1)S(1)}, u32[]{:S(2)}, u32[]{:S(2)}) async-start(bf16[128,48,128]{2,1,0:T(8,128)(2,1)} %get-tuple-element.13), calls=%async_computation.1 | async-start | bytes 3145728 | tf_op jit(solution)/shard_map/all_to_all | solution.py:761
  134.4 29.9 %copy-start = (bf16[128,48,128]{2,1,0:T(8,128)(2,1)}, bf16[128,48,128]{2,1,0:T(8,128)(2,1)S(1)}, u32[]{:S(2)}) copy-start(bf16[128,48,128]{2,1,0:T(8,128)(2,1)S(1)} %all-to-all-done.1.first_hbm) | copy-start | bytes 4718596
